TPU v7x, 128 devices: a whole 4x4x4 slice. The times are simulated.
128 devices in a mesh: section: 2 (over core), rows: 8 (over x, y_lo), cols: 8 (over y_hi, z).
Axes of the slice: x: 4, y: 4 (y_hi: 2, y_lo: 2; y = y_hi * 2 + y_lo), z: 4, core: 2. Of those that a mesh axis runs over, the one named last changes fastest.
Arguments:
- tensor_data: bfloat16 [1024, 16, 32768], P('rows', 'section', 'cols'), may hold values from 0 to 3
- matrix_data: bfloat16 [1024, 32768], P('rows', ('cols', 'section')), may hold values from 0 to 3
- word_factor: bfloat16 [300, 1024], P(None, 'rows'), may hold values from -2.5 to 2.5
- context_factor: bfloat16 [300, 32768], P(None, 'cols'), may hold values from -2.5 to 2.5
- offset_factor: bfloat16 [300, 16], P(None, 'section'), may hold values from -2.5 to 2.5
Outputs:
- grad_word: float32 [300, 1024], P(None, 'rows')
- grad_context: float32 [300, 32768], P(None, ('cols', 'section', 'rows'))
- grad_offset: float32 [300, 16], P(None, 'section')
All inputs are finite; a program needn't handle non-finite values.
Results may differ from a plain program's by a relative error of at most 0.0012.
Values sent between devices are 32-bit elements; how exact they have to be, the bound alone decides.
No kernel may reach another device: no remote copies, remote signals or barrier semaphores. Data moves between devices by JAX's collectives and lax.ppermute only.
A program may use at most 256 MiB of HBM per device.

v0:
```python
import math

import jax
import jax.numpy as jnp
from jax import lax
from jax.sharding import PartitionSpec as P


def contract_first(left, right):
    return lax.dot_general(
        left, right, (((0,), (0,)), ((), ())), preferred_element_type=jnp.float32
    )


def contract_last(left, right):
    return lax.dot_general(
        left, right, (((1,), (1,)), ((), ())), preferred_element_type=jnp.float32
    )


def per_device(tensor_data, matrix_data, word_factor, context_factor, offset_factor):
    local_rows, offset_width, context_width = tensor_data.shape
    rank_count = word_factor.shape[0]
    total_words = local_rows * lax.axis_size("rows")
    total_offsets = offset_width * lax.axis_size("section")
    total_contexts = context_width * lax.axis_size("cols")
    offset_wide = offset_factor.astype(jnp.float32)
    context_wide = context_factor.astype(jnp.float32)
    paired = (offset_wide[:, :, None] * context_wide[:, None, :]).astype(jnp.bfloat16)
    paired = paired.reshape(rank_count, offset_width * context_width)
    unfolded = tensor_data.reshape(local_rows, offset_width * context_width)
    fitted = contract_first(word_factor, paired)
    residual = (fitted - unfolded.astype(jnp.float32)).astype(jnp.bfloat16)
    word_tensor = contract_last(paired, residual)
    weighted = jnp.dot(word_factor, residual, preferred_element_type=jnp.float32)
    weighted = weighted.reshape(rank_count, offset_width, context_width)
    context_tensor = jnp.sum(weighted * offset_wide[:, :, None], axis=1)
    offset_partial = jnp.sum(weighted * context_wide[:, None, :], axis=2)
    matrix_width = matrix_data.shape[1]
    begin_col = lax.axis_index("section") * matrix_width
    context_slice = lax.dynamic_slice_in_dim(context_factor, begin_col, matrix_width, 1)
    fitted_matrix = contract_first(word_factor, context_slice)
    residual_matrix = (fitted_matrix - matrix_data.astype(jnp.float32)).astype(jnp.bfloat16)
    word_matrix = contract_last(context_slice, residual_matrix)
    context_matrix = jnp.dot(word_factor, residual_matrix, preferred_element_type=jnp.float32)
    word_total = lax.psum(word_tensor + word_matrix, ("section", "cols"))
    offset_total = lax.psum(offset_partial, ("rows", "cols"))
    padded_matrix = lax.dynamic_update_slice_in_dim(
        jnp.zeros((rank_count, context_width), jnp.float32), context_matrix, begin_col, 1
    )
    context_total = lax.psum_scatter(
        context_tensor + padded_matrix, ("section", "rows"), scatter_dimension=1, tiled=True
    )
    grad_word = word_total / math.sqrt(total_contexts * total_offsets)
    grad_context = context_total / math.sqrt(total_words * total_offsets)
    grad_offset = offset_total / math.sqrt(total_words * total_contexts)
    return (grad_word, grad_context, grad_offset)


def solution(mesh):
    return jax.shard_map(
        per_device,
        mesh=mesh,
        in_specs=(
            P("rows", "section", "cols"),
            P("rows", ("cols", "section")),
            P(None, "rows"),
            P(None, "cols"),
            P(None, "section"),
        ),
        out_specs=(P(None, "rows"), P(None, ("cols", "section", "rows")), P(None, "section")),
        check_vma=False,
    )
```

profile of v0, /device:TPU:0, one launch (start us, length us, event | category | flops | bytes accessed | tf_op | source)
XLA Modules:
  0.0 534.1 jit_solution(110045387927039498)
XLA Ops:
  8.0 0.0 copy-start
  8.0 0.0 all-reduce.2.cloned.1.call-start
  8.1 0.8 copy.11
  8.9 2.1 copy.13
  10.9 4.5 convert_element_type.29
  15.4 14.0 %copy.12 = f32[128,8,4096]{0,2,1:T(8,128)} copy(bf16[128,8,4096]{2,1,0:T(8,128)(2,1)} %param.5) | data formatting | bytes 25165824 | tf_op jit(solution)/shard_map/convert_element_type | solution.py:33
  29.5 8.2 %multiply_convert_fusion = bf16[300,8,4096]{2,1,0:T(8,128)(2,1)S(1)} fusion(f32[300,4096]{1,0:T(8,128)} %convert_element_type.29, f32[300,8]{1,0:T(8,128)S(1)} %copy.11), kind=kLoop, calls=%fused_computation.3 | loop fusion | flops 19660800 | bytes 24585600 | tf_op jit(solution)/shard_map/convert_element_type | solution.py:29
  37.7 2.8 pad
  40.5 12.8 %copy.15 = bf16[38,8,8,4096]{3,1,2,0:T(8,128)(2,1)} copy(bf16[38,8,8,4096]{3,2,1,0:T(8,128)(2,1)S(1)} %bitcast.41) | data formatting | bytes 39845888
  53.4 18.6 %fusion.1 = bf16[128,32768]{0,1:T(8,128)(2,1)} fusion(f32[128,32768]{0,1:T(8,128)} %bitcast.40, bf16[300,32768]{1,0:T(8,128)(2,1)} %bitcast.36, bf16[300,128]{1,0:T(8,128)(2,1)S(1)} %copy-done), kind=kOutput, calls=%fused_computation.5 | convolution fusion | flops 2524971008 | bytes 44903424 | tf_op jit(solution)/shard_map/dot_general | solution.py:10
  72.0 12.1 %fusion.10 = f32[300,128]{1,0:T(8,128)S(1)} fusion(bf16[300,32768]{1,0:T(8,128)(2,1)} %bitcast.37, bf16[128,32768]{0,1:T(8,128)(2,1)} %fusion.1), kind=kOutput, calls=%fused_computation.20 | convolution fusion | flops 2516582400 | bytes 28203008 | tf_op jit(solution)/shard_map/dot_general | solution.py:16
  84.1 1.7 fusion.5
  85.8 1.2 convolution_add_fusion
  87.0 0.0 all-reduce.2.cloned.1.call-update
  87.0 0.2 reduce-scatter.2.cloned.1.call-start
  87.3 21.8 %fusion.11 = f32[32768,300]{0,1:T(8,128)} fusion(bf16[128,32768]{0,1:T(8,128)(2,1)} %fusion.1, bf16[300,128]{1,0:T(8,128)(2,1)S(1)} %copy-done), kind=kOutput, calls=%fused_computation.21 | convolution fusion | flops 2516582400 | bytes 47787008 | tf_op jit(solution)/shard_map/dot_general | solution.py:35
  109.0 37.9 %copy.16 = f32[38,8,8,4096]{3,2,1,0:T(8,128)} copy(f32[38,8,8,4096]{3,1,2,0:T(8,128)} %bitcast.38) | data formatting | bytes 79691776
  146.9 21.6 %multiply_reduce_fusion = (f32[300,8]{1,0:T(8,128)S(1)}, f32[300,4096]{1,0:T(8,128)}) fusion(f32[304,8,4096]{2,1,0:T(8,128)} %bitcast.39, f32[300,4096]{1,0:T(8,128)} %convert_element_type.29, f32[300,8]{1,0:T(8,128)S(1)} %copy.11), kind=kLoop, calls=%fused_computation.1 | loop fusion | flops 38090400 | bytes 49171200 | tf_op jit(solution)/shard_map/reduce_sum | solution.py:38
  168.6 3.6 fusion.3
  172.2 0.0 reduce-scatter.2.cloned.1.call-update
  172.2 350.5 %psum.15 = f32[300,8]{1,0:T(8,128)S(1)} all-reduce(f32[300,8]{1,0:T(8,128)S(1)} %get-tuple-element.6), channel_id=1, replica_groups=mesh['section'=2,'rows'=8,'cols'=8] {'rows','cols'}, use_global_device_ids=true, to_apply=%region_4.0 | all-reduce | flops 2400 | bytes 19200 | tf_op jit(solution)/shard_map/psum | solution.py:47
  522.7 0.7 copy.14
  523.4 1.6 broadcast_multiply_fusion.2
  525.0 1.7 broadcast_multiply_fusion
  (6 shorter events, 0.0 us)
Async XLA Ops:
  8.0 45.4 %copy-start = (bf16[300,128]{1,0:T(8,128)(2,1)S(1)}, bf16[300,128]{1,0:T(8,128)(2,1)}, u32[]{:S(2)}) copy-start(bf16[300,128]{1,0:T(8,128)(2,1)} %param.7) | copy-start | bytes 230404
  8.0 515.4 %all-reduce.2.cloned.1.call-start = ((), (), s32[]{:S(2)}) async-start(), calls=%async_computation.1 | async-start | bytes 311296 | tf_op jit(solution)/shard_map/psum | solution.py:46
  72.0 12.1 %copy-start.1 = (bf16[300,4096]{1,0:T(8,128)(2,1)S(1)}, bf16[300,4096]{1,0:T(8,128)(2,1)}, u32[]{:S(2)}) copy-start(bf16[300,4096]{1,0:T(8,128)(2,1)} %param.8) | copy-start | bytes 7372804
  87.0 438.0 %reduce-scatter.2.cloned.1.call-start = ((), (), s32[]{:S(2)}) async-start(), calls=%async_computation.2 | async-start | bytes 5292032 | tf_op jit(solution)/shard_map/reduce_scatter | solution.py:51
Sparse Core Ops, SparseCore 0:
  87.1 164.5 all-reduce.1
Sparse Core Ops, SparseCore 1:
  172.3 115.6 reduce-scatter.1
where the time goes:
time: 535 us; the launch traced here: 534 us
  blocking collectives  350 us (65%)
  local copies, waits for them, and re-layouts  71.2 us (13%)
  matrix products  59 us (11%)
  other arithmetic  37.7 us (7%)
  between operations  15.5 us (3%)
    psum x1, blocking collectives, per_device(): offset_total = lax.psum(offset_partial, ('rows', 'cols'))  350 us
    unnamed x9, local copies, waits for them, and re-layouts  56.3 us
    dot_general x1, matrix products, per_device(): jnp.dot(word_factor, residual, preferred_element_type=jnp.float32)  21.8 us
    reduce_sum x1, other arithmetic, per_device(): offset_partial = jnp.sum(weighted * context_wide[:, None, :], axis=2)  21.6 us
    dot_general x2, matrix products, contract_first(): lax.dot_general(left, right, (((0,), (0,)), ((), ())), preferred_element_...  20.3 us
    convert_element_type x1, local copies, waits for them, and re-layouts, per_device(): residual = (fitted - unfolded.astype(jnp.float32)).astype(jnp.bfloat16)  14 us
    dot_general x2, matrix products, contract_last(): lax.dot_general(left, right, (((1,), (1,)), ((), ())), preferred_element_...  13.3 us
  transfers between devices with their start and end apart: 2, of which 0 were waited for; matrix products, arithmetic and copies ran while one was open for 16% of the time, Pallas kernels for 0%

commit v1 on v0

v1 whole, which is shorter than its diff:
```python
import functools
import math

import jax
import jax.numpy as jnp
from jax import lax
from jax.experimental import pallas as pl
from jax.experimental.pallas import tpu as pltpu
from jax.sharding import PartitionSpec as P

F32 = jnp.float32
BF16 = jnp.bfloat16
MIB = 1024 * 1024
NT = (((1,), (1,)), ((), ()))
TN = (((0,), (0,)), ((), ()))


def dot(a, b):
    return jnp.dot(a, b, preferred_element_type=F32)


def dot_nt(a, b):
    return lax.dot_general(a, b, NT, preferred_element_type=F32)


def dot_tn(a, b):
    return lax.dot_general(a, b, TN, preferred_element_type=F32)


def split_two(v):
    hi = v.astype(BF16)
    return hi, (v - hi.astype(F32)).astype(BF16)


def word_spread(words, offsets):
    n = words * offsets
    col = lax.broadcasted_iota(jnp.int32, (words, n), 1)
    row = lax.broadcasted_iota(jnp.int32, (words, n), 0)
    inside = (col >= row * offsets) & (col < row * offsets + offsets)
    return jnp.where(inside, 1.0, 0.0).astype(BF16)


def offset_spread(words, offsets):
    n = words * offsets
    col = lax.broadcasted_iota(jnp.int32, (offsets, n), 1)
    row = lax.broadcasted_iota(jnp.int32, (offsets, n), 0)
    return jnp.where(lax.rem(col, offsets) == row, 1.0, 0.0).astype(BF16)


def context_kernel(own, pos_ref, word_ref, off_ref, data_ref, ctx_ref, mat_ref, out_ref, a_ref, hi_ref, lo_ref):
    words, offsets = word_ref.shape[1], off_ref.shape[0]

    @pl.when(pl.program_id(0) == 0)
    def _():
        w = word_ref[...]
        o = off_ref[...]
        wide_w = dot(w, word_spread(words, offsets))
        wide_o = dot_tn(o, offset_spread(words, offsets))
        a_ref[...] = (wide_w * wide_o).astype(BF16)
        gram = dot_tn(o, o)
        if own:
            gram = gram + 1.0
        hi, lo = split_two(dot_nt(w, w) * gram)
        hi_ref[...] = hi
        lo_ref[...] = lo

    c = ctx_ref[...]
    acc = dot(hi_ref[...], c) + dot(lo_ref[...], c) - dot(a_ref[...], data_ref[...])
    if own:
        acc = acc - dot(word_ref[...], mat_ref[...])
    out_ref[...] = acc


def context_part(own, pos, data, matrix, word, off_t, ctx):
    rank, words = word.shape
    offsets = off_t.shape[0]
    rows, width = data.shape
    half = width // 2
    tile = 512
    steps = half // tile

    def column(i, pos):
        which = pos[0] if own else 1 - pos[0]
        return (0, which * steps + i)

    grid_spec = pltpu.PrefetchScalarGridSpec(
        num_scalar_prefetch=1,
        grid=(steps,),
        in_specs=[
            pl.BlockSpec((rank, words), lambda i, pos: (0, 0)),
            pl.BlockSpec((offsets, rank), lambda i, pos: (0, 0)),
            pl.BlockSpec((rows, tile), column),
            pl.BlockSpec((rank, tile), column),
            pl.BlockSpec((words, tile), (lambda i, pos: (0, i)) if own else (lambda i, pos: (0, 0))),
        ],
        out_specs=pl.BlockSpec((rank, tile), lambda i, pos: (0, i)),
        scratch_shapes=[
            pltpu.VMEM((rank, rows), BF16),
            pltpu.VMEM((rank, rank), BF16),
            pltpu.VMEM((rank, rank), BF16),
        ],
    )
    flops = 2 * rank * half * (rows + 2 * rank)
    return pl.pallas_call(
        functools.partial(context_kernel, own),
        out_shape=jax.ShapeDtypeStruct((rank, half), F32),
        grid_spec=grid_spec,
        compiler_params=pltpu.CompilerParams(vmem_limit_bytes=24 * MIB),
        cost_estimate=pl.CostEstimate(flops=flops, bytes_accessed=rows * half * 2 + rank * half * 6, transcendentals=0),
        name="context_own" if own else "context_other",
    )(pos, word, off_t, data, ctx, matrix)


def word_kernel(pos_ref, word_ref, off_ref, data_ref, ctx_ref, mat_ref, word_out, off_out, b_ref, m_ref, c0_ref, c1_ref):
    i = pl.program_id(0)
    steps = pl.num_programs(0)
    words, offsets = word_ref.shape[1], off_ref.shape[0]
    rank = word_ref.shape[0]
    section = pos_ref[0]

    @pl.when(i == 0)
    def _():
        b_ref[...] = jnp.zeros_like(b_ref)
        m_ref[...] = jnp.zeros_like(m_ref)
        c0_ref[...] = jnp.zeros_like(c0_ref)
        c1_ref[...] = jnp.zeros_like(c1_ref)

    c = ctx_ref[...]
    b_ref[...] += dot_nt(c, data_ref[...])
    gram = dot_nt(c, c)
    mine = (i >= section * (steps // 2)) & (i < (section + 1) * (steps // 2))

    @pl.when(mine)
    def _():
        m_ref[...] += dot_nt(c, mat_ref[...])
        c0_ref[...] += gram

    @pl.when(jnp.logical_not(mine))
    def _():
        c1_ref[...] += gram

    @pl.when(i == steps - 1)
    def _():
        w = word_ref[...]
        o = off_ref[...]
        spread_w = word_spread(words, offsets)
        spread_o = offset_spread(words, offsets)
        b = b_ref[...]
        own = c0_ref[...]
        both = own + c1_ref[...]
        n_hi, n_lo = split_two(dot_tn(o, o) * both + own)
        b_hi, b_lo = split_two(b * dot_tn(o, spread_o))
        total = dot(n_hi, w) + dot(n_lo, w) - m_ref[...]
        total = total - dot_nt(b_hi, spread_w) - dot_nt(b_lo, spread_w)
        word_out[...] = jnp.zeros_like(word_out)
        word_out[pl.ds(0, rank), :] = total
        p_hi, p_lo = split_two(dot_nt(w, w) * both)
        v_hi, v_lo = split_two(b * dot(w, spread_w))
        off = dot(o, p_hi) + dot(o, p_lo) - dot_nt(spread_o, v_hi) - dot_nt(spread_o, v_lo)
        off_out[...] = jnp.zeros_like(off_out)
        for k in range(off_out.shape[0] // offsets):
            lanes = min(128, rank - k * 128)
            off_out[pl.ds(k * offsets, offsets), pl.ds(0, lanes)] = off[:, k * 128 : k * 128 + lanes]


def word_part(pos, data, matrix, word, off_t, ctx):
    rank, words = word.shape
    offsets = off_t.shape[0]
    rows, width = data.shape
    tile = 512
    steps = width // tile
    padded = -(-rank // 16) * 16
    chunks = -(-rank // 128)

    def mat_column(i, pos):
        return (0, jnp.clip(i - pos[0] * (steps // 2), 0, steps // 2 - 1))

    grid_spec = pltpu.PrefetchScalarGridSpec(
        num_scalar_prefetch=1,
        grid=(steps,),
        in_specs=[
            pl.BlockSpec((rank, words), lambda i, pos: (0, 0)),
            pl.BlockSpec((offsets, rank), lambda i, pos: (0, 0)),
            pl.BlockSpec((rows, tile), lambda i, pos: (0, i)),
            pl.BlockSpec((rank, tile), lambda i, pos: (0, i)),
            pl.BlockSpec((words, tile), mat_column),
        ],
        out_specs=[
            pl.BlockSpec((padded, words), lambda i, pos: (0, 0)),
            pl.BlockSpec((chunks * offsets, 128), lambda i, pos: (0, 0)),
        ],
        scratch_shapes=[
            pltpu.VMEM((rank, rows), F32),
            pltpu.VMEM((rank, words), F32),
            pltpu.VMEM((rank, rank), F32),
            pltpu.VMEM((rank, rank), F32),
        ],
    )
    return pl.pallas_call(
        word_kernel,
        out_shape=[
            jax.ShapeDtypeStruct((padded, words), F32),
            jax.ShapeDtypeStruct((chunks * offsets, 128), F32),
        ],
        grid_spec=grid_spec,
        compiler_params=pltpu.CompilerParams(vmem_limit_bytes=24 * MIB),
        cost_estimate=pl.CostEstimate(
            flops=2 * rank * width * (rows + rank), bytes_accessed=rows * width * 2 + rank * width * 2, transcendentals=0
        ),
        name="word_offset",
    )(pos, word, off_t, data, ctx, matrix)


def whole_call(kernel, outs, name, pos, *args):
    vmem = pl.BlockSpec(memory_space=pltpu.VMEM)
    total = sum(a.size for a in args) * 4 + sum(math.prod(o) for o in outs) * 4
    return pl.pallas_call(
        kernel,
        out_shape=[jax.ShapeDtypeStruct(o, F32) for o in outs],
        in_specs=[pl.BlockSpec(memory_space=pltpu.SMEM)] + [vmem] * len(args),
        out_specs=[vmem] * len(outs),
        compiler_params=pltpu.CompilerParams(vmem_limit_bytes=24 * MIB),
        cost_estimate=pl.CostEstimate(flops=total // 4, bytes_accessed=total, transcendentals=0),
        name=name,
    )(pos, *args)


def lanes(start, width):
    return pl.ds(pl.multiple_of(start, 128), width)


def first_sum(top, pos_ref, own_ref, got_ref, x1_ref, x2_ref, x3_ref, y_ref, kx_ref, ky_ref):
    x, y = pos_ref[1], pos_ref[2]
    rank = own_ref.shape[0]
    block = ky_ref.shape[1] // 4
    upper, lower = pl.ds(0, top), pl.ds(top, rank - top)
    for hop, ref in ((1, x1_ref), (2, x2_ref), (3, x3_ref), (0, kx_ref)):
        at = lanes(lax.rem(x + hop, 4) * (2 * block), 2 * block)
        ref[...] = own_ref[upper, at] + got_ref[upper, at]
    for side, ref in ((1 - y, y_ref), (y, ky_ref)):
        for k in range(4):
            at = lanes((2 * k + side) * block, block)
            ref[:, pl.ds(k * block, block)] = own_ref[lower, at] + got_ref[lower, at]


def x_sum(pos_ref, k_ref, a_ref, b_ref, c_ref, send_ref, keep_ref):
    y = pos_ref[2]
    block = send_ref.shape[1]
    for side, ref in ((1 - y, send_ref), (y, keep_ref)):
        at = lanes(side * block, block)
        ref[...] = (k_ref[:, at] + a_ref[:, at]) + (b_ref[:, at] + c_ref[:, at])


def y_sum(pos_ref, k_ref, a_ref, x1_ref, x2_ref, x3_ref, keep_ref):
    x = pos_ref[1]
    block = keep_ref.shape[1]
    for hop, ref in ((1, x1_ref), (2, x2_ref), (3, x3_ref), (0, keep_ref)):
        at = lanes(lax.rem(x + hop, 4) * block, block)
        ref[...] = k_ref[:, at] + a_ref[:, at]


def last_sum(scale, pos_ref, k_ref, a_ref, l_ref, b_ref, c_ref, d_ref, out_ref):
    top = k_ref.shape[0]
    rank = out_ref.shape[0]
    out_ref[pl.ds(0, top), :] = (k_ref[...] + a_ref[...]) * scale
    out_ref[pl.ds(top, rank - top), :] = ((l_ref[...] + b_ref[...]) + (c_ref[...] + d_ref[...])) * scale


def rows_perm(move):
    pairs = []
    for x in range(4):
        for y in range(2):
            nx, ny = move(x, y)
            pairs.append((x * 2 + y, (nx % 4) * 2 + ny % 2))
    return pairs


def cols_perm(move):
    pairs = []
    for y in range(2):
        for z in range(4):
            ny, nz = move(y, z)
            pairs.append((y * 4 + z, (ny % 2) * 4 + nz % 4))
    return pairs


X_HOP = {h: rows_perm(lambda x, y, h=h: (x + h, y)) for h in (1, 2, 3)}
Y_LOW = rows_perm(lambda x, y: (x, 1 - y))
Z_HOP = {h: cols_perm(lambda y, z, h=h: (y, z + h)) for h in (1, 2, 3)}
Y_HIGH = cols_perm(lambda y, z: (1 - y, z))
SWAP = [(0, 1), (1, 0)]


def send(v, axis, perm):
    return lax.ppermute(v, axis, perm)


def ring_sum(v, axis, hops):
    a, b, c = (send(v, axis, hops[h]) for h in (1, 2, 3))
    return (v + b) + (a + c)


def per_device(tensor_data, matrix_data, word_factor, context_factor, offset_factor):
    words, offsets, width = tensor_data.shape
    rank = word_factor.shape[0]
    all_words = words * lax.axis_size("rows")
    all_offsets = offsets * lax.axis_size("section")
    all_contexts = width * lax.axis_size("cols")
    section = lax.axis_index("section")
    row = lax.axis_index("rows")
    pos = jnp.stack([section, row // 2, row % 2]).astype(jnp.int32)
    data = tensor_data.reshape(words * offsets, width)
    off_t = offset_factor.T
    args = (pos, data, matrix_data, word_factor, off_t, context_factor)

    other = context_part(False, *args)
    got = send(other, "section", SWAP)
    own = context_part(True, *args)

    top = -(-rank // 16) * 8
    low = rank - top
    block = width // 16
    x1, x2, x3, y1, kx, ky = whole_call(
        functools.partial(first_sum, top),
        [(top, 2 * block)] * 3 + [(low, 4 * block), (top, 2 * block), (low, 4 * block)],
        "first_sum", pos, own, got,
    )
    f2 = send(x2, "rows", X_HOP[2])
    f1 = send(x1, "rows", X_HOP[1])
    f3 = send(x3, "rows", X_HOP[3])
    g = send(y1, "rows", Y_LOW)
    sx, kx = whole_call(x_sum, [(top, block)] * 2, "x_sum", pos, kx, f1, f2, f3)
    x1, x2, x3, ky = whole_call(y_sum, [(low, block)] * 4, "y_sum", pos, ky, g)
    f2 = send(x2, "rows", X_HOP[2])
    f1 = send(x1, "rows", X_HOP[1])
    f3 = send(x3, "rows", X_HOP[3])
    g = send(sx, "rows", Y_LOW)
    scale = 1.0 / math.sqrt(all_words * all_offsets)
    (grad_context,) = whole_call(
        functools.partial(last_sum, scale), [(rank, block)], "last_sum", pos, kx, g, ky, f1, f2, f3
    )

    word_own, off_own = word_part(*args)
    part = word_own.shape[0] // 2
    away = lax.dynamic_slice_in_dim(word_own, (1 - section) * part, part, 0)
    home = lax.dynamic_slice_in_dim(word_own, section * part, part, 0)
    home = home + send(away, "section", SWAP)
    both = jnp.concatenate([home, off_own], axis=0)
    both = ring_sum(both, "cols", Z_HOP)
    both = both + send(both, "cols", Y_HIGH)
    home = both[:part]
    away = send(home, "section", SWAP)
    first = jnp.where(section == 0, home, away)
    second = jnp.where(section == 0, away, home)
    grad_word = jnp.concatenate([first, second], axis=0)[:rank] / math.sqrt(all_contexts * all_offsets)
    off = ring_sum(both[part:], "rows", X_HOP)
    off = off + send(off, "rows", Y_LOW)
    off = jnp.concatenate([off[k * offsets : (k + 1) * offsets] for k in range(off.shape[0] // offsets)], axis=1)
    grad_offset = (off[:, :rank] / math.sqrt(all_words * all_contexts)).T
    return (grad_word, grad_context, grad_offset)


def solution(mesh):
    return jax.shard_map(
        per_device,
        mesh=mesh,
        in_specs=(
            P("rows", "section", "cols"),
            P("rows", ("cols", "section")),
            P(None, "rows"),
            P(None, "cols"),
            P(None, "section"),
        ),
        out_specs=(P(None, "rows"), P(None, ("cols", "section", "rows")), P(None, "section")),
        check_vma=False,
    )
```

time: 535 us -> 98.7 us (0.18)
  blocking collectives: 350 us -> 0 us
  matrix products: 59 us -> 0 us
  local copies, waits for them, and re-layouts: 71.2 us -> 14.5 us
  other arithmetic: 37.7 us -> 1.45 us
  starting transfers between devices: 0.26 us -> 31.4 us
  Pallas kernels: 0 us -> 25.9 us
  waiting for transfers between devices: 0.04 us -> 24.2 us
  between operations: 15.5 us -> 0.8 us
    psum x1 -> x0, blocking collectives: 350 us -> none  [per_device(): offset_total = lax.psum(offset_partial, ('rows', 'cols'))]
    dot_general x6 -> x0, matrix products: 59 us -> none  [the longest x1 21.8 us: per_device(): jnp.dot(word_factor, residual, preferred_element_type=jnp.float32)]
    unnamed x9 -> x22, local copies, waits for them, and re-layouts: 56.3 us -> 14.5 us
    ppermute x0 -> x19, starting transfers between devices: none -> 31.4 us  [send(): return lax.ppermute(v, axis, perm)]
    pallas_call x0 -> x7, Pallas kernels: none -> 25.9 us  [the longest x2 11.3 us: context_part(): pl.pallas_call(functools.partial(context_kernel, own), out_shape=jax.Shap...]
    ppermute x0 -> x19, waiting for transfers between devices: none -> 24.2 us  [send(): return lax.ppermute(v, axis, perm)]
    reduce_sum x1 -> x0, other arithmetic: 21.6 us -> none  [per_device(): offset_partial = jnp.sum(weighted * context_wide[:, None, :], axis=2)]
    convert_element_type x2 -> x0, local copies, waits for them, and re-layouts: 14.8 us -> none  [the longest x1 14 us: per_device(): residual = (fitted - unfolded.astype(jnp.float32)).astype(jnp.bfloat16)]
  transfers between devices with their start and end apart: 2 -> 19, of which waited for: 0 -> 9; matrix products, arithmetic and copies ran while one was open for 16% -> 1% of each run, Pallas kernels for 0% -> 19%
where the time goes in v1:
time: 98.7 us; the launch traced here: 98.3 us
  starting transfers between devices  31.4 us (32%)
  Pallas kernels  25.9 us (26%)
  waiting for transfers between devices  24.2 us (25%)
  local copies, waits for them, and re-layouts  14.5 us (15%)
  other arithmetic  1.45 us (1%)
    ppermute x19, starting transfers between devices, send(): return lax.ppermute(v, axis, perm)  31.4 us
    ppermute x19, waiting for transfers between devices, send(): return lax.ppermute(v, axis, perm)  24.2 us
    unnamed x22, local copies, waits for them, and re-layouts  14.5 us
    pallas_call x2, Pallas kernels, context_part(): pl.pallas_call(functools.partial(context_kernel, own), out_shape=jax.Shap...  11.3 us
    pallas_call x1, Pallas kernels, word_part(): pl.pallas_call(word_kernel, out_shape=[jax.ShapeDtypeStruct((padded, word...  9.97 us
    pallas_call x4, Pallas kernels, whole_call(): pl.pallas_call(kernel, out_shape=[jax.ShapeDtypeStruct(o, F32) for o in o...  4.62 us
  transfers between devices with their start and end apart: 19, of which 9 were waited for; matrix products, arithmetic and copies ran while one was open for 1% of the time, Pallas kernels for 19%

profile of v1, /device:TPU:0, one launch (start us, length us, event | category | flops | bytes accessed | tf_op | source)
XLA Modules:
  0.0 98.3 jit_solution(2629086626956041052)
XLA Ops:
  0.7 3.4 %copy-done = bf16[128,8,4096]{2,1,0:T(8,128)(2,1)S(1)} copy-done((bf16[128,8,4096]{2,1,0:T(8,128)(2,1)S(1)}, bf16[128,8,4096]{2,1,0:T(8,128)(2,1)}, u32[]{:S(2)}) %copy-start) | copy-done | bytes 8388632
  4.1 1.7 %copy-done.3 = bf16[300,4096]{1,0:T(8,128)(2,1)S(1)} copy-done((bf16[300,4096]{1,0:T(8,128)(2,1)S(1)}, bf16[300,4096]{1,0:T(8,128)(2,1)}, u32[]{:S(2)}) %copy-start.3) | copy-done | bytes 2457624
  8.4 5.8 %context_other.1 = f32[300,2048]{1,0:T(8,128)} custom-call(s32[3]{0:T(128)S(1)} %pad_add_fusion.pos_ref, bf16[300,128]{1,0:T(8,128)(2,1)S(1)} %copy-done.7, bf16[8,300]{1,0:T(8,128)(2,1)S(1)} %bitcast.10, bf16[1024,4096]{1,0:T(8,128)(2,1)S(1)} %bitcast.7, bf16[300,4096]{1,0:T(8,128)(2,1)S(1)} %copy-done.3, bf16[128,2048]{1,0:T(8,128)(2,1)S(1)} %copy-done.5), custom_call_target="tpu_custom_call" | custom-call | flops 1995571200 | bytes 7880704 | tf_op jit(solution)/shard_map/context_other/pallas_call | solution.py:104
  14.3 3.4 %copy-done.1 = bf16[128,8,4096]{2,1,0:T(8,128)(2,1)S(1)} copy-done((bf16[128,8,4096]{2,1,0:T(8,128)(2,1)S(1)}, bf16[128,8,4096]{2,1,0:T(8,128)(2,1)}, u32[]{:S(2)}) %copy-start.1) | copy-done | bytes 8388632
  17.7 10.0 %word_offset.1 = (f32[304,128]{1,0:T(8,128)S(1)}, f32[24,128]{1,0:T(8,128)S(1)}) custom-call(s32[3]{0:T(128)S(1)} %pad_add_fusion.pos_ref, bf16[300,128]{1,0:T(8,128)(2,1)S(1)} %copy-done.8, bf16[8,300]{1,0:T(8,128)(2,1)S(1)} %bitcast.11, bf16[1024,4096]{1,0:T(8,128)(2,1)S(1)} %bitcast.8, bf16[300,4096]{1,0:T(8,128)(2,1)S(1)} %copy-done.4, ...), custom_call_target="tpu_custom_call" | custom-call | flops 3253862400 | bytes 10846208 | tf_op jit(solution)/shard_map/word_offset/pallas_call | solution.py:199
  29.2 4.0 %collective-permute-start.1 = (f32[176,128]{1,0:T(8,128)S(1)}, f32[176,128]{1,0:T(8,128)S(1)}, u32[]{:S(2)}, u32[]{:S(2)}) collective-permute-start(f32[176,128]{1,0:T(8,128)S(1)} %pad_maximum_fusion.1), channel_id=1, source_target_pairs={{0,2},{1,3},{2,0},{3,1},{4,6},{5,7},{6,4},{7,5},{8,10},{9,11},{10,... | collective-permute-start | bytes 270344 | tf_op jit(solution)/shard_map/ppermute | solution.py:295
  34.3 2.2 %collective-permute-start.3 = (f32[176,128]{1,0:T(8,128)S(1)}, f32[176,128]{1,0:T(8,128)S(1)}, u32[]{:S(2)}, u32[]{:S(2)}) collective-permute-start(f32[176,128]{1,0:T(8,128)S(1)} %pad_maximum_fusion.1), channel_id=1, source_target_pairs={{0,3},{1,0},{2,1},{3,2},{4,7},{5,4},{6,5},{7,6},{8,11},{9,8},{10,9... | collective-permute-start | bytes 270344 | tf_op jit(solution)/shard_map/ppermute | solution.py:295
  36.7 2.4 %collective-permute-done.2 = f32[176,128]{1,0:T(8,128)S(1)} collective-permute-done((f32[176,128]{1,0:T(8,128)S(1)}, f32[176,128]{1,0:T(8,128)S(1)}, u32[]{:S(2)}, u32[]{:S(2)}) %collective-permute-start.2) | collective-permute-done | bytes 90144 | tf_op jit(solution)/shard_map/ppermute | solution.py:295
  39.1 3.3 %collective-permute-start.4 = (f32[176,128]{1,0:T(8,128)S(1)}, f32[176,128]{1,0:T(8,128)S(1)}, u32[]{:S(2)}, u32[]{:S(2)}) collective-permute-start(f32[176,128]{1,0:T(8,128)S(1)} %add_add_fusion), channel_id=1, source_target_pairs={{0,4},{1,5},{2,6},{3,7},{4,0},{5,1},{6,2},{7,3},{8,12},{9,13},{10,... | collective-permute-start | bytes 270344 | tf_op jit(solution)/shard_map/ppermute | solution.py:295
  42.4 3.4 %copy-done.2 = bf16[128,8,4096]{2,1,0:T(8,128)(2,1)S(1)} copy-done((bf16[128,8,4096]{2,1,0:T(8,128)(2,1)S(1)}, bf16[128,8,4096]{2,1,0:T(8,128)(2,1)}, u32[]{:S(2)}) %copy-start.2) | copy-done | bytes 8388632
  45.7 5.5 %context_own.1.own_ref = f32[300,2048]{1,0:T(8,128)S(1)} custom-call(s32[3]{0:T(128)S(1)} %pad_add_fusion.pos_ref, bf16[300,128]{1,0:T(8,128)(2,1)S(1)} %copy-done.8, bf16[8,300]{1,0:T(8,128)(2,1)S(1)} %bitcast.12, bf16[1024,4096]{1,0:T(8,128)(2,1)S(1)} %bitcast.9, bf16[300,4096]{1,0:T(8,128)(2,1)S(1)} %copy-done.4, bf16[128,2048]{1,0:T(8,128)(2,1)S(1)} %copy-done.6), custom_call_target="tpu_custom_call" | custom-call | flops 1995571200 | bytes 7880704 | tf_op jit(solution)/shard_map/context_own/pallas_call | solution.py:104
  51.3 2.0 %first_sum.1 = (f32[152,512]{1,0:T(8,128)S(1)}, f32[152,512]{1,0:T(8,128)S(1)}, f32[152,512]{1,0:T(8,128)S(1)}, f32[148,1024]{1,0:T(8,128)S(1)}, f32[152,512]{1,0:T(8,128)S(1)}, /*index=5*/f32[148,1024]{1,0:T(8,128)S(1)}) custom-call(s32[3]{0:T(128)S(1)} %pad_add_fusion.pos_ref, f32[300,2048]{1,0:T(8,128)S(1)} %context_own.1.own_ref, ...), custom_call_target="tpu_custom_call" | custom-call | flops 1843200 | bytes 7372800 | tf_op jit(solution)/shard_map/first_sum/pallas_call | solution.py:217
  54.1 3.1 %collective-permute-start.15 = (f32[24,128]{1,0:T(8,128)S(1)}, f32[24,128]{1,0:T(8,128)S(1)}, u32[]{:S(2)}, u32[]{:S(2)}) collective-permute-start(f32[24,128]{1,0:T(8,128)S(1)} %slice.29), channel_id=1, source_target_pairs={{0,32},{8,40},{16,48},{24,56},{32,0},{40,8},{48,16},{56,24},{1,33}... | collective-permute-start | bytes 36872 | tf_op jit(solution)/shard_map/ppermute | solution.py:295
  57.8 2.7 %collective-permute-start.17 = (f32[24,128]{1,0:T(8,128)S(1)}, f32[24,128]{1,0:T(8,128)S(1)}, u32[]{:S(2)}, u32[]{:S(2)}) collective-permute-start(f32[24,128]{1,0:T(8,128)S(1)} %slice.29), channel_id=1, source_target_pairs={{0,48},{8,56},{16,0},{24,8},{32,16},{40,24},{48,32},{56,40},{1,49}... | collective-permute-start | bytes 36872 | tf_op jit(solution)/shard_map/ppermute | solution.py:295
  60.4 1.7 %collective-permute-done.16 = f32[24,128]{1,0:T(8,128)S(1)} collective-permute-done((f32[24,128]{1,0:T(8,128)S(1)}, f32[24,128]{1,0:T(8,128)S(1)}, u32[]{:S(2)}, u32[]{:S(2)}) %collective-permute-start.16) | collective-permute-done | bytes 12320 | tf_op jit(solution)/shard_map/ppermute | solution.py:295
  63.6 5.1 %collective-permute-done.18 = f32[24,128]{1,0:T(8,128)S(1)} collective-permute-done((f32[24,128]{1,0:T(8,128)S(1)}, f32[24,128]{1,0:T(8,128)S(1)}, u32[]{:S(2)}, u32[]{:S(2)}) %collective-permute-start.18) | collective-permute-done | bytes 12320 | tf_op jit(solution)/shard_map/ppermute | solution.py:295
  68.7 1.5 %collective-permute-start.7 = (f32[152,512]{1,0:T(8,128)S(1)}, f32[152,512]{1,0:T(8,128)S(1)}, u32[]{:S(2)}, u32[]{:S(2)}) collective-permute-start(f32[152,512]{1,0:T(8,128)S(1)} %get-tuple-element.20), channel_id=1, source_target_pairs={{0,16},{8,24},{16,32},{24,40},{32,48},{40,56},{48,0},{56,8},{1,17}... | collective-permute-start | bytes 933896 | tf_op jit(solution)/shard_map/ppermute | solution.py:295
  70.2 2.7 %collective-permute-start.8 = (f32[152,512]{1,0:T(8,128)S(1)}, f32[152,512]{1,0:T(8,128)S(1)}, u32[]{:S(2)}, u32[]{:S(2)}) collective-permute-start(f32[152,512]{1,0:T(8,128)S(1)} %get-tuple-element.21), channel_id=1, source_target_pairs={{0,32},{8,40},{16,48},{24,56},{32,0},{40,8},{48,16},{56,24},{1,33}... | collective-permute-start | bytes 933896 | tf_op jit(solution)/shard_map/ppermute | solution.py:295
  74.9 4.3 %collective-permute-done.7.a_ref = f32[152,512]{1,0:T(8,128)S(1)} collective-permute-done((f32[152,512]{1,0:T(8,128)S(1)}, f32[152,512]{1,0:T(8,128)S(1)}, u32[]{:S(2)}, u32[]{:S(2)}) %collective-permute-start.7) | collective-permute-done | bytes 311328 | tf_op jit(solution)/shard_map/ppermute | solution.py:295
  79.2 5.8 %collective-permute-done.8.b_ref = f32[152,512]{1,0:T(8,128)S(1)} collective-permute-done((f32[152,512]{1,0:T(8,128)S(1)}, f32[152,512]{1,0:T(8,128)S(1)}, u32[]{:S(2)}, u32[]{:S(2)}) %collective-permute-start.8) | collective-permute-done | bytes 311328 | tf_op jit(solution)/shard_map/ppermute | solution.py:295
  88.4 2.4 %collective-permute-start.13 = (f32[148,256]{1,0:T(8,128)S(1)}, f32[148,256]{1,0:T(8,128)S(1)}, u32[]{:S(2)}, u32[]{:S(2)}) collective-permute-start(f32[148,256]{1,0:T(8,128)S(1)} %get-tuple-element.29), channel_id=1, source_target_pairs={{0,32},{8,40},{16,48},{24,56},{32,0},{40,8},{48,16},{56,24},{1,33}... | collective-permute-start | bytes 454664 | tf_op jit(solution)/shard_map/ppermute | solution.py:295
  90.8 1.6 %collective-permute-start.14 = (f32[148,256]{1,0:T(8,128)S(1)}, f32[148,256]{1,0:T(8,128)S(1)}, u32[]{:S(2)}, u32[]{:S(2)}) collective-permute-start(f32[148,256]{1,0:T(8,128)S(1)} %get-tuple-element.30), channel_id=1, source_target_pairs={{0,48},{8,56},{16,0},{24,8},{32,16},{40,24},{48,32},{56,40},{1,49}... | collective-permute-start | bytes 454664 | tf_op jit(solution)/shard_map/ppermute | solution.py:295
  93.1 2.1 %collective-permute-done.12.b_ref = f32[148,256]{1,0:T(8,128)S(1)} collective-permute-done((f32[148,256]{1,0:T(8,128)S(1)}, f32[148,256]{1,0:T(8,128)S(1)}, u32[]{:S(2)}, u32[]{:S(2)}) %collective-permute-start.12) | collective-permute-done | bytes 151584 | tf_op jit(solution)/shard_map/ppermute | solution.py:295
  95.2 1.8 %collective-permute-done.13.c_ref = f32[148,256]{1,0:T(8,128)S(1)} collective-permute-done((f32[148,256]{1,0:T(8,128)S(1)}, f32[148,256]{1,0:T(8,128)S(1)}, u32[]{:S(2)}, u32[]{:S(2)}) %collective-permute-start.13) | collective-permute-done | bytes 151584 | tf_op jit(solution)/shard_map/ppermute | solution.py:295
  (57 shorter events, 15.8 us)
Async XLA Ops:
  8.4 5.8 %copy-start.4 = (bf16[300,4096]{1,0:T(8,128)(2,1)S(1)}, bf16[300,4096]{1,0:T(8,128)(2,1)}, u32[]{:S(2)}) copy-start(bf16[300,4096]{1,0:T(8,128)(2,1)} %ctx_ref.5) | copy-start | bytes 7372804
  8.4 5.8 %copy-start.6 = (bf16[128,2048]{1,0:T(8,128)(2,1)S(1)}, bf16[128,2048]{1,0:T(8,128)(2,1)}, u32[]{:S(2)}) copy-start(bf16[128,2048]{1,0:T(8,128)(2,1)} %mat_ref.5) | copy-start | bytes 1572868
  8.4 5.8 %copy-start.8 = (bf16[300,128]{1,0:T(8,128)(2,1)S(1)}, bf16[300,128]{1,0:T(8,128)(2,1)}, u32[]{:S(2)}) copy-start(bf16[300,128]{1,0:T(8,128)(2,1)} %word_ref.5) | copy-start | bytes 230404
  8.4 5.8 %copy-start.10 = (bf16[300,8]{0,1:T(8,128)(2,1)S(1)}, bf16[300,8]{0,1:T(8,128)(2,1)}, u32[]{:S(2)}) copy-start(bf16[300,8]{0,1:T(8,128)(2,1)} %param.9) | copy-start | bytes 14404
  14.3 37.0 %collective-permute-start.6 = (f32[300,2048]{1,0:T(8,128)}, f32[300,2048]{1,0:T(8,128)}, u32[]{:S(2)}, u32[]{:S(2)}) collective-permute-start(f32[300,2048]{1,0:T(8,128)} %context_other.1), channel_id=1, source_target_pairs={{0,64},{64,0},{1,65},{65,1},{2,66},{66,2},{3,67},{67,3},{4,68},{68... | collective-permute-start | bytes 7372808 | tf_op jit(solution)/shard_map/ppermute | solution.py:295
  14.3 3.4 %copy-start.1 = (bf16[128,8,4096]{2,1,0:T(8,128)(2,1)S(1)}, bf16[128,8,4096]{2,1,0:T(8,128)(2,1)}, u32[]{:S(2)}) copy-start(bf16[128,8,4096]{2,1,0:T(8,128)(2,1)} %param.5) | copy-start | bytes 25165828
  27.7 1.5 %collective-permute-start = (f32[152,128]{1,0:T(8,128)S(1)}, f32[152,128]{1,0:T(8,128)S(1)}, u32[]{:S(2)}, u32[]{:S(2)}) collective-permute-start(f32[152,128]{1,0:T(8,128)S(1)} %constant_dynamic-slice_fusion), channel_id=1, source_target_pairs={{0,64},{64,0},{1,65},{65,1},{2,66},{66,2},{3,67},{67,3},{4,68},{68... | collective-permute-start | bytes 233480 | tf_op jit(solution)/shard_map/ppermute | solution.py:295
  29.2 7.5 %collective-permute-start.1 = (f32[176,128]{1,0:T(8,128)S(1)}, f32[176,128]{1,0:T(8,128)S(1)}, u32[]{:S(2)}, u32[]{:S(2)}) collective-permute-start(f32[176,128]{1,0:T(8,128)S(1)} %pad_maximum_fusion.1), channel_id=1, source_target_pairs={{0,2},{1,3},{2,0},{3,1},{4,6},{5,7},{6,4},{7,5},{8,10},{9,11},{10,... | collective-permute-start | bytes 270344 | tf_op jit(solution)/shard_map/ppermute | solution.py:295
  33.2 5.8 %collective-permute-start.2 = (f32[176,128]{1,0:T(8,128)S(1)}, f32[176,128]{1,0:T(8,128)S(1)}, u32[]{:S(2)}, u32[]{:S(2)}) collective-permute-start(f32[176,128]{1,0:T(8,128)S(1)} %pad_maximum_fusion.1), channel_id=1, source_target_pairs={{0,1},{1,2},{2,3},{3,0},{4,5},{5,6},{6,7},{7,4},{8,9},{9,10},{10,1... | collective-permute-start | bytes 270344 | tf_op jit(solution)/shard_map/ppermute | solution.py:295
  34.3 4.8 %collective-permute-start.3 = (f32[176,128]{1,0:T(8,128)S(1)}, f32[176,128]{1,0:T(8,128)S(1)}, u32[]{:S(2)}, u32[]{:S(2)}) collective-permute-start(f32[176,128]{1,0:T(8,128)S(1)} %pad_maximum_fusion.1), channel_id=1, source_target_pairs={{0,3},{1,0},{2,1},{3,2},{4,7},{5,4},{6,5},{7,6},{8,11},{9,8},{10,9... | collective-permute-start | bytes 270344 | tf_op jit(solution)/shard_map/ppermute | solution.py:295
  39.1 15.0 %collective-permute-start.4 = (f32[176,128]{1,0:T(8,128)S(1)}, f32[176,128]{1,0:T(8,128)S(1)}, u32[]{:S(2)}, u32[]{:S(2)}) collective-permute-start(f32[176,128]{1,0:T(8,128)S(1)} %add_add_fusion), channel_id=1, source_target_pairs={{0,4},{1,5},{2,6},{3,7},{4,0},{5,1},{6,2},{7,3},{8,12},{9,13},{10,... | collective-permute-start | bytes 270344 | tf_op jit(solution)/shard_map/ppermute | solution.py:295
  53.3 33.1 %collective-permute-start.11 = (f32[148,1024]{1,0:T(8,128)S(1)}, f32[148,1024]{1,0:T(8,128)S(1)}, u32[]{:S(2)}, u32[]{:S(2)}) collective-permute-start(f32[148,1024]{1,0:T(8,128)S(1)} %get-tuple-element.26), channel_id=1, source_target_pairs={{0,8},{8,0},{16,24},{24,16},{32,40},{40,32},{48,56},{56,48},{1,9},... | collective-permute-start | bytes 1818632 | tf_op jit(solution)/shard_map/ppermute | solution.py:295
  54.1 6.3 %collective-permute-start.15 = (f32[24,128]{1,0:T(8,128)S(1)}, f32[24,128]{1,0:T(8,128)S(1)}, u32[]{:S(2)}, u32[]{:S(2)}) collective-permute-start(f32[24,128]{1,0:T(8,128)S(1)} %slice.29), channel_id=1, source_target_pairs={{0,32},{8,40},{16,48},{24,56},{32,0},{40,8},{48,16},{56,24},{1,33}... | collective-permute-start | bytes 36872 | tf_op jit(solution)/shard_map/ppermute | solution.py:295
  57.2 4.9 %collective-permute-start.16 = (f32[24,128]{1,0:T(8,128)S(1)}, f32[24,128]{1,0:T(8,128)S(1)}, u32[]{:S(2)}, u32[]{:S(2)}) collective-permute-start(f32[24,128]{1,0:T(8,128)S(1)} %slice.29), channel_id=1, source_target_pairs={{0,16},{8,24},{16,32},{24,40},{32,48},{40,56},{48,0},{56,8},{1,17}... | collective-permute-start | bytes 36872 | tf_op jit(solution)/shard_map/ppermute | solution.py:295
  57.8 4.3 %collective-permute-start.17 = (f32[24,128]{1,0:T(8,128)S(1)}, f32[24,128]{1,0:T(8,128)S(1)}, u32[]{:S(2)}, u32[]{:S(2)}) collective-permute-start(f32[24,128]{1,0:T(8,128)S(1)} %slice.29), channel_id=1, source_target_pairs={{0,48},{8,56},{16,0},{24,8},{32,16},{40,24},{48,32},{56,40},{1,49}... | collective-permute-start | bytes 36872 | tf_op jit(solution)/shard_map/ppermute | solution.py:295
  62.1 6.6 %collective-permute-start.18 = (f32[24,128]{1,0:T(8,128)S(1)}, f32[24,128]{1,0:T(8,128)S(1)}, u32[]{:S(2)}, u32[]{:S(2)}) collective-permute-start(f32[24,128]{1,0:T(8,128)S(1)} %add_add_fusion.1), channel_id=1, source_target_pairs={{0,8},{8,0},{16,24},{24,16},{32,40},{40,32},{48,56},{56,48},{1,9},... | collective-permute-start | bytes 36872 | tf_op jit(solution)/shard_map/ppermute | solution.py:295
  63.6 28.8 %collective-permute-start.5 = (f32[152,128]{1,0:T(8,128)S(1)}, f32[152,128]{1,0:T(8,128)S(1)}, u32[]{:S(2)}, u32[]{:S(2)}) collective-permute-start(f32[152,128]{1,0:T(8,128)S(1)} %slice.28), channel_id=1, source_target_pairs={{0,64},{64,0},{1,65},{65,1},{2,66},{66,2},{3,67},{67,3},{4,68},{68... | collective-permute-start | bytes 233480 | tf_op jit(solution)/shard_map/ppermute | solution.py:295
  68.7 10.5 %collective-permute-start.7 = (f32[152,512]{1,0:T(8,128)S(1)}, f32[152,512]{1,0:T(8,128)S(1)}, u32[]{:S(2)}, u32[]{:S(2)}) collective-permute-start(f32[152,512]{1,0:T(8,128)S(1)} %get-tuple-element.20), channel_id=1, source_target_pairs={{0,16},{8,24},{16,32},{24,40},{32,48},{40,56},{48,0},{56,8},{1,17}... | collective-permute-start | bytes 933896 | tf_op jit(solution)/shard_map/ppermute | solution.py:295
  70.2 14.8 %collective-permute-start.8 = (f32[152,512]{1,0:T(8,128)S(1)}, f32[152,512]{1,0:T(8,128)S(1)}, u32[]{:S(2)}, u32[]{:S(2)}) collective-permute-start(f32[152,512]{1,0:T(8,128)S(1)} %get-tuple-element.21), channel_id=1, source_target_pairs={{0,32},{8,40},{16,48},{24,56},{32,0},{40,8},{48,16},{56,24},{1,33}... | collective-permute-start | bytes 933896 | tf_op jit(solution)/shard_map/ppermute | solution.py:295
  72.9 12.1 %collective-permute-start.9 = (f32[152,512]{1,0:T(8,128)S(1)}, f32[152,512]{1,0:T(8,128)S(1)}, u32[]{:S(2)}, u32[]{:S(2)}) collective-permute-start(f32[152,512]{1,0:T(8,128)S(1)} %get-tuple-element.22), channel_id=1, source_target_pairs={{0,48},{8,56},{16,0},{24,8},{32,16},{40,24},{48,32},{56,40},{1,49}... | collective-permute-start | bytes 933896 | tf_op jit(solution)/shard_map/ppermute | solution.py:295
  85.6 7.5 %collective-permute-start.10 = (f32[152,256]{1,0:T(8,128)S(1)}, f32[152,256]{1,0:T(8,128)S(1)}, u32[]{:S(2)}, u32[]{:S(2)}) collective-permute-start(f32[152,256]{1,0:T(8,128)S(1)} %get-tuple-element.24), channel_id=1, source_target_pairs={{0,8},{8,0},{16,24},{24,16},{32,40},{40,32},{48,56},{56,48},{1,9},... | collective-permute-start | bytes 466952 | tf_op jit(solution)/shard_map/ppermute | solution.py:295
  87.0 8.2 %collective-permute-start.12 = (f32[148,256]{1,0:T(8,128)S(1)}, f32[148,256]{1,0:T(8,128)S(1)}, u32[]{:S(2)}, u32[]{:S(2)}) collective-permute-start(f32[148,256]{1,0:T(8,128)S(1)} %get-tuple-element.28), channel_id=1, source_target_pairs={{0,16},{8,24},{16,32},{24,40},{32,48},{40,56},{48,0},{56,8},{1,17}... | collective-permute-start | bytes 454664 | tf_op jit(solution)/shard_map/ppermute | solution.py:295
  88.4 8.6 %collective-permute-start.13 = (f32[148,256]{1,0:T(8,128)S(1)}, f32[148,256]{1,0:T(8,128)S(1)}, u32[]{:S(2)}, u32[]{:S(2)}) collective-permute-start(f32[148,256]{1,0:T(8,128)S(1)} %get-tuple-element.29), channel_id=1, source_target_pairs={{0,32},{8,40},{16,48},{24,56},{32,0},{40,8},{48,16},{56,24},{1,33}... | collective-permute-start | bytes 454664 | tf_op jit(solution)/shard_map/ppermute | solution.py:295
  90.8 6.2 %collective-permute-start.14 = (f32[148,256]{1,0:T(8,128)S(1)}, f32[148,256]{1,0:T(8,128)S(1)}, u32[]{:S(2)}, u32[]{:S(2)}) collective-permute-start(f32[148,256]{1,0:T(8,128)S(1)} %get-tuple-element.30), channel_id=1, source_target_pairs={{0,48},{8,56},{16,0},{24,8},{32,16},{40,24},{48,32},{56,40},{1,49}... | collective-permute-start | bytes 454664 | tf_op jit(solution)/shard_map/ppermute | solution.py:295
  (6 other events, 11.1 us)

commit v2 on v0

v2 whole, which is shorter than its diff:
```python
import functools
import math

import jax
import jax.numpy as jnp
from jax import lax
from jax.experimental import pallas as pl
from jax.experimental.pallas import tpu as pltpu
from jax.sharding import PartitionSpec as P

F32 = jnp.float32
BF16 = jnp.bfloat16
MIB = 1024 * 1024
BIG = 50 * MIB
OWN = 42 * MIB
WORD = 50 * MIB
FRONT_TILE = 512
TOP = 160
NT = (((1,), (1,)), ((), ()))
TN = (((0,), (0,)), ((), ()))


def dot(a, b):
    return jnp.dot(a, b, preferred_element_type=F32)


def dot_nt(a, b):
    return lax.dot_general(a, b, NT, preferred_element_type=F32)


def dot_tn(a, b):
    return lax.dot_general(a, b, TN, preferred_element_type=F32)


def split_two(v):
    hi = v.astype(BF16)
    return hi, (v - hi.astype(F32)).astype(BF16)


def chunk_count(rank):
    return -(-rank // 128)


def word_spread(words, offsets):
    n = words * offsets
    col = lax.broadcasted_iota(jnp.int32, (words, n), 1)
    row = lax.broadcasted_iota(jnp.int32, (words, n), 0)
    inside = (col >= row * offsets) & (col < row * offsets + offsets)
    return jnp.where(inside, 1.0, 0.0).astype(BF16)


def offset_spread(words, offsets):
    n = words * offsets
    col = lax.broadcasted_iota(jnp.int32, (offsets, n), 1)
    row = lax.broadcasted_iota(jnp.int32, (offsets, n), 0)
    return jnp.where(lax.rem(col, offsets) == row, 1.0, 0.0).astype(BF16)


def start_loads(plan):
    steps = []
    for parts in plan:
        copies = [pltpu.make_async_copy(*p) for p in parts]
        for c in copies:
            c.start()
        steps.append(copies)
    return steps


def front_kernel(pos_ref, word_ref, off_ref, data_ref, ctx_ref, mat_ref, *refs):
    ctx_out, a_out, out_ref, d_buf, c_buf, m_buf, d_sem, c_sem, m_sem = refs
    steps, _, tile = d_buf.shape
    words, offsets = word_ref.shape[1], off_ref.shape[0]
    rank = word_ref.shape[0]
    section = pos_ref[0]
    half = steps // 2
    plan = []
    for i in range(steps):
        side = 1 - section if i < half else section
        at = lanes((side * half + i % half) * tile, tile)
        plan.append([(ctx_ref.at[:, at], c_buf.at[i], c_sem.at[i]), (data_ref.at[:, at], d_buf.at[i], d_sem.at[i])])
        if i >= half:
            k = i - half
            plan[-1].append((mat_ref.at[:, pl.ds(k * tile, tile)], m_buf.at[k], m_sem.at[k]))
    loads = start_loads(plan)
    w = word_ref[...]
    o = off_ref[...]
    spread_w = word_spread(words, offsets)
    spread_o = offset_spread(words, offsets)
    wide_w = dot(w, spread_w)
    wide_o = dot_tn(o, spread_o)
    a = (wide_w * wide_o).astype(BF16)
    a_out[...] = a
    gram_w = dot_nt(w, w)
    gram_o = dot_tn(o, o)
    m_hi, m_lo = split_two(gram_w * gram_o)
    b = m = own = other = None

    def plus(total, term):
        return term if total is None else total + term

    for i in range(steps):
        for c in loads[i]:
            c.wait()
        c = c_buf[i]
        gram = dot_nt(c, c)
        if i < half:
            ctx_out[:, pl.ds(i * tile, tile)] = dot(m_hi, c) + dot(m_lo, c) - dot(a, d_buf[i])
            other = plus(other, gram)
        else:
            m = plus(m, dot_nt(c, m_buf[i - half]))
            own = plus(own, gram)
        b = plus(b, dot_nt(c, d_buf[i]))

    both = own + other
    n_hi, n_lo = split_two(gram_o * both + own)
    b_hi, b_lo = split_two(b * wide_o)
    total = dot(n_hi, w) + dot(n_lo, w) - m
    total = total - dot_nt(b_hi, spread_w) - dot_nt(b_lo, spread_w)
    low = out_ref.shape[0] - chunk_count(rank) * offsets
    out_ref[pl.ds(0, rank), :] = total
    out_ref[pl.ds(rank, low - rank), :] = jnp.zeros((low - rank, words), F32)
    p_hi, p_lo = split_two(gram_w * both)
    v_hi, v_lo = split_two(b * wide_w)
    off = dot_nt(p_hi, o) + dot_nt(p_lo, o) - dot_nt(v_hi, spread_o) - dot_nt(v_lo, spread_o)
    off = off.T
    for k in range(chunk_count(rank)):
        part = min(128, rank - k * 128)
        at = pl.ds(low + k * offsets, offsets)
        out_ref[at, :] = jnp.zeros((offsets, 128), F32)
        out_ref[at, pl.ds(0, part)] = off[:, k * 128 : k * 128 + part]


def front_part(pos, data, matrix, word, off_t, ctx):
    rank, words = word.shape
    offsets = off_t.shape[0]
    rows, width = data.shape
    tile = min(FRONT_TILE, width // 2)
    steps = width // tile
    half = steps // 2
    out_rows = -(-rank // 8) * 8 + chunk_count(rank) * offsets
    vmem = pl.BlockSpec(memory_space=pltpu.VMEM)
    anywhere = pl.BlockSpec(memory_space=pl.ANY)
    return pl.pallas_call(
        front_kernel,
        out_shape=[
            jax.ShapeDtypeStruct((rank, width // 2), F32),
            jax.ShapeDtypeStruct((rank, rows), BF16),
            jax.ShapeDtypeStruct((out_rows, words), F32),
        ],
        in_specs=[pl.BlockSpec(memory_space=pltpu.SMEM), vmem, vmem] + [anywhere] * 3,
        out_specs=[vmem] * 3,
        scratch_shapes=[
            pltpu.VMEM((steps, rows, tile), BF16),
            pltpu.VMEM((steps, rank, tile), BF16),
            pltpu.VMEM((half, words, tile), BF16),
            pltpu.SemaphoreType.DMA((steps,)),
            pltpu.SemaphoreType.DMA((steps,)),
            pltpu.SemaphoreType.DMA((half,)),
        ],
        compiler_params=pltpu.CompilerParams(vmem_limit_bytes=WORD),
        cost_estimate=pl.CostEstimate(
            flops=3 * rank * width * (rows + rank), bytes_accessed=rows * width * 2 + rank * width * 2, transcendentals=0
        ),
        name="front",
    )(pos, word, off_t, data, ctx, matrix)


def own_kernel(pos_ref, word_ref, off_ref, a_ref, data_ref, ctx_ref, mat_ref, after_ref, out_ref, *refs):
    del after_ref
    d_buf, c_buf, m_buf, d_sem, c_sem, m_sem = refs
    steps, _, tile = d_buf.shape
    base = pos_ref[0] * (steps * tile)
    plan = []
    for i in range(steps):
        here = pl.ds(i * tile, tile)
        there = lanes(base + i * tile, tile)
        plan.append([
            (ctx_ref.at[:, there], c_buf.at[i], c_sem.at[i]),
            (mat_ref.at[:, here], m_buf.at[i], m_sem.at[i]),
            (data_ref.at[:, there], d_buf.at[i], d_sem.at[i]),
        ])
    loads = start_loads(plan)
    w = word_ref[...]
    o = off_ref[...]
    a = a_ref[...]
    hi, lo = split_two(dot_nt(w, w) * (dot_tn(o, o) + 1.0))
    for i in range(steps):
        for c in loads[i]:
            c.wait()
        total = dot(hi, c_buf[i]) + dot(lo, c_buf[i]) - dot(w, m_buf[i]) - dot(a, d_buf[i])
        out_ref[:, pl.ds(i * tile, tile)] = total


def own_part(pos, data, matrix, word, off_t, ctx, a, after):
    rank, words = word.shape
    rows, width = data.shape
    half = width // 2
    tile = min(512, half)
    steps = half // tile
    vmem = pl.BlockSpec(memory_space=pltpu.VMEM)
    anywhere = pl.BlockSpec(memory_space=pl.ANY)
    flops = 100 * rank * half * (rows + 2 * rank)
    return pl.pallas_call(
        own_kernel,
        out_shape=jax.ShapeDtypeStruct((rank, half), F32),
        in_specs=[pl.BlockSpec(memory_space=pltpu.SMEM), vmem, vmem, vmem] + [anywhere] * 4,
        out_specs=vmem,
        scratch_shapes=[
            pltpu.VMEM((steps, rows, tile), BF16),
            pltpu.VMEM((steps, rank, tile), BF16),
            pltpu.VMEM((steps, words, tile), BF16),
        ]
        + [pltpu.SemaphoreType.DMA((steps,))] * 3,
        compiler_params=pltpu.CompilerParams(vmem_limit_bytes=OWN),
        cost_estimate=pl.CostEstimate(flops=flops, bytes_accessed=rows * half * 100 + rank * half * 300, transcendentals=0),
        name="own_half",
    )(pos, word, off_t, a, data, ctx, matrix, after)


def whole_call(kernel, outs, name, pos, *args, after=()):
    vmem = pl.BlockSpec(memory_space=pltpu.VMEM)
    anywhere = pl.BlockSpec(memory_space=pl.ANY)
    n = 1 + len(args)

    def body(*refs):
        kernel(*refs[:n], *refs[n + len(after) :])

    return pl.pallas_call(
        body,
        out_shape=[jax.ShapeDtypeStruct(o, F32) for o in outs],
        in_specs=[pl.BlockSpec(memory_space=pltpu.SMEM)] + [vmem] * len(args) + [anywhere] * len(after),
        out_specs=[vmem] * len(outs),
        compiler_params=pltpu.CompilerParams(vmem_limit_bytes=24 * MIB),
        cost_estimate=pl.CostEstimate(flops=1024, bytes_accessed=1024, transcendentals=0),
        name=name,
    )(pos, *args, *after)


def lanes(start, width):
    return pl.ds(pl.multiple_of(start, 128), width)


def first_sum(pos_ref, own_ref, got_ref, x1_ref, x2_ref, x3_ref, y_ref, kx_ref, ky_ref):
    x, y = pos_ref[1], pos_ref[2]
    top, width = kx_ref.shape
    low, span = ky_ref.shape
    block = span // 4
    for hop, ref in ((1, x1_ref), (3, x3_ref), (2, x2_ref), (0, kx_ref)):
        at = lanes(lax.rem(x + hop, 4) * width, width)
        ref[...] = own_ref[pl.ds(0, top), at] + got_ref[pl.ds(0, top), at]
    for side, ref in ((1 - y, y_ref), (y, ky_ref)):
        for k in range(4):
            at = lanes((2 * k + side) * block, block)
            ref[:, pl.ds(k * block, block)] = own_ref[pl.ds(top, low), at] + got_ref[pl.ds(top, low), at]


def middle_sum(pos_ref, k_ref, a_ref, b_ref, c_ref, l_ref, g_ref, off_ref, more_ref, *refs):
    sx_ref, kx_ref, x1_ref, x2_ref, x3_ref, ky_ref = refs
    x, y = pos_ref[1], pos_ref[2]
    block = sx_ref.shape[1]
    low = l_ref.shape[0]
    for hop, ref in ((1, x1_ref), (3, x3_ref), (2, x2_ref), (0, ky_ref)):
        at = lanes(lax.rem(x + hop, 4) * block, block)
        ref[pl.ds(0, low), :] = l_ref[:, at] + g_ref[:, at]
    begin = -(-low // 8) * 8
    extra = ky_ref.shape[0] - begin
    total = off_ref[...] + more_ref[...]
    for ref in (x1_ref, x2_ref, x3_ref, ky_ref):
        if begin > low:
            ref[pl.ds(low, begin - low), :] = jnp.zeros((begin - low, block), F32)
        ref[pl.ds(begin, extra), pl.ds(0, 128)] = total
        ref[pl.ds(begin, extra), pl.ds(128, block - 128)] = jnp.zeros((extra, block - 128), F32)
    for side, ref in ((1 - y, sx_ref), (y, kx_ref)):
        at = lanes(side * block, block)
        ref[...] = (k_ref[:, at] + a_ref[:, at]) + (b_ref[:, at] + c_ref[:, at])


def last_sum(scales, pos_ref, k_ref, a_ref, l_ref, b_ref, c_ref, d_ref, w_ref, v_ref, ctx_ref, word_ref, off_ref):
    top = k_ref.shape[0]
    rank = ctx_ref.shape[0]
    low = rank - top
    ctx_ref[pl.ds(0, top), :] = (k_ref[...] + a_ref[...]) * scales[0]
    rows = pl.ds(0, low)
    ctx_ref[pl.ds(top, low), :] = ((l_ref[rows, :] + c_ref[rows, :]) + (b_ref[rows, :] + d_ref[rows, :])) * scales[0]
    word_ref[...] = (w_ref[pl.ds(0, rank), :] + v_ref[pl.ds(0, rank), :]) * scales[1]
    end = -(-low // 8) * 8
    offsets = off_ref.shape[0]
    for k in range(chunk_count(rank)):
        at = pl.ds(end + k * offsets, offsets)
        part = min(128, rank - k * 128)
        total = (l_ref[at, :] + c_ref[at, :]) + (b_ref[at, :] + d_ref[at, :])
        off_ref[:, pl.ds(k * 128, part)] = total[:, :part] * scales[2]


def rows_perm(move):
    pairs = []
    for x in range(4):
        for y in range(2):
            nx, ny = move(x, y)
            pairs.append((x * 2 + y, (nx % 4) * 2 + ny % 2))
    return pairs


def cols_perm(move):
    pairs = []
    for y in range(2):
        for z in range(4):
            ny, nz = move(y, z)
            pairs.append((y * 4 + z, (ny % 2) * 4 + nz % 4))
    return pairs


X_HOP = {h: rows_perm(lambda x, y, h=h: (x + h, y)) for h in (1, 2, 3)}
Y_LOW = rows_perm(lambda x, y: (x, 1 - y))
Z_PAIR = [cols_perm(lambda y, z, h=h: (y, z ^ h)) for h in (1, 2)]
Y_HIGH = cols_perm(lambda y, z: (1 - y, z))
SWAP = [(0, 1), (1, 0)]


def send(v, axis, perm):
    return lax.ppermute(v, axis, perm)


def per_device(tensor_data, matrix_data, word_factor, context_factor, offset_factor):
    words, offsets, width = tensor_data.shape
    rank = word_factor.shape[0]
    all_words = words * lax.axis_size("rows")
    all_offsets = offsets * lax.axis_size("section")
    all_contexts = width * lax.axis_size("cols")
    section = lax.axis_index("section")
    row = lax.axis_index("rows")
    pos = jnp.stack([section, row // 2, row % 2]).astype(jnp.int32)
    data = tensor_data.reshape(words * offsets, width)
    off_t = offset_factor.T
    other, a, part = front_part(pos, data, matrix_data, word_factor, off_t, context_factor)
    got = send(other, "section", SWAP)
    z1 = send(part, "cols", Z_PAIR[0])
    own = own_part(pos, data, matrix_data, word_factor, off_t, context_factor, a, part)
    part = part + z1
    z2 = send(part, "cols", Z_PAIR[1])

    top = TOP
    low = rank - top
    block = width // 16
    extra = chunk_count(rank) * offsets
    x1, x2, x3, y1, kx, ky = whole_call(
        first_sum, [(top, 2 * block)] * 3 + [(low, 4 * block), (top, 2 * block), (low, 4 * block)],
        "first_sum", pos, own, got, after=(part,),
    )
    f1 = send(x1, "rows", X_HOP[1])
    f3 = send(x3, "rows", X_HOP[3])
    g = send(y1, "rows", Y_LOW)
    f2 = send(x2, "rows", X_HOP[2])
    never = row < 0
    part = part + z2
    part = jnp.where(never, f1[:1, :1], part)
    word = part + send(part, "cols", Y_HIGH)
    off = word[word.shape[0] - extra :]
    more = send(off, "rows", Y_LOW)
    longer = (-(-low // 8) * 8 + extra, block)
    sx, kx, x1, x2, x3, ky = whole_call(
        middle_sum, [(top, block)] * 2 + [longer] * 4, "middle_sum", pos, kx, f1, f2, f3, ky, g, off, more
    )
    f1 = send(x1, "rows", X_HOP[1])
    f3 = send(x3, "rows", X_HOP[3])
    f2 = send(x2, "rows", X_HOP[2])
    g = send(sx, "rows", Y_LOW)
    other_word = send(word, "section", SWAP)
    scales = (
        1.0 / math.sqrt(all_words * all_offsets),
        1.0 / math.sqrt(all_contexts * all_offsets),
        1.0 / math.sqrt(all_words * all_contexts),
    )
    grad_context, grad_word, grad_offset = whole_call(
        functools.partial(last_sum, scales),
        [(rank, block), (rank, words), (offsets, rank)],
        "last_sum", pos, kx, g, ky, f1, f2, f3, word, other_word,
    )
    return (grad_word, grad_context, grad_offset.T)


def solution(mesh):
    return jax.shard_map(
        per_device,
        mesh=mesh,
        in_specs=(
            P("rows", "section", "cols"),
            P("rows", ("cols", "section")),
            P(None, "rows"),
            P(None, "cols"),
            P(None, "section"),
        ),
        out_specs=(P(None, "rows"), P(None, ("cols", "section", "rows")), P(None, "section")),
        check_vma=False,
    )
```

time: 535 us -> 69 us (0.13)
  blocking collectives: 350 us -> 0 us
  local copies, waits for them, and re-layouts: 71.2 us -> 3.15 us
  matrix products: 59 us -> 0 us
  other arithmetic: 37.7 us -> 0.79 us
  starting transfers between devices: 0.26 us -> 22.1 us
  waiting for transfers between devices: 0.04 us -> 21 us
  Pallas kernels: 0 us -> 20.3 us
  between operations: 15.5 us -> 0.76 us
    psum x1 -> x0, blocking collectives: 350 us -> none  [per_device(): offset_total = lax.psum(offset_partial, ('rows', 'cols'))]
    dot_general x6 -> x0, matrix products: 59 us -> none  [the longest x1 21.8 us: per_device(): jnp.dot(word_factor, residual, preferred_element_type=jnp.float32)]
    unnamed x9 -> x14, local copies, waits for them, and re-layouts: 56.3 us -> 2.63 us
    ppermute x0 -> x14, starting transfers between devices: none -> 22.1 us  [send(): return lax.ppermute(v, axis, perm)]
    reduce_sum x1 -> x0, other arithmetic: 21.6 us -> none  [per_device(): offset_partial = jnp.sum(weighted * context_wide[:, None, :], axis=2)]
    ppermute x0 -> x14, waiting for transfers between devices: none -> 21 us  [send(): return lax.ppermute(v, axis, perm)]
    pallas_call x0 -> x5, Pallas kernels: none -> 20.3 us  [the longest x1 11.9 us: front_part(): pl.pallas_call(front_kernel, out_shape=[jax.ShapeDtypeStruct((rank, width...]
    convert_element_type x2 -> x0, local copies, waits for them, and re-layouts: 14.8 us -> none  [the longest x1 14 us: per_device(): residual = (fitted - unfolded.astype(jnp.float32)).astype(jnp.bfloat16)]
  transfers between devices with their start and end apart: 2 -> 14, of which waited for: 0 -> 5; matrix products, arithmetic and copies ran while one was open for 16% -> 2% of each run, Pallas kernels for 0% -> 8%
where the time goes in v2:
time: 69 us; the launch traced here: 68.1 us
  starting transfers between devices  22.1 us (32%)
  waiting for transfers between devices  21 us (30%)
  Pallas kernels  20.3 us (29%)
  local copies, waits for them, and re-layouts  3.15 us (5%)
  other arithmetic  0.79 us (1%)
  between operations  0.76 us (1%)
    ppermute x14, starting transfers between devices, send(): return lax.ppermute(v, axis, perm)  22.1 us
    ppermute x14, waiting for transfers between devices, send(): return lax.ppermute(v, axis, perm)  21 us
    pallas_call x1, Pallas kernels, front_part(): pl.pallas_call(front_kernel, out_shape=[jax.ShapeDtypeStruct((rank, width...  11.9 us
    pallas_call x1, Pallas kernels, own_part(): pl.pallas_call(own_kernel, out_shape=jax.ShapeDtypeStruct((rank, half), F...  5.49 us
    pallas_call x3, Pallas kernels, whole_call(): pl.pallas_call(body, out_shape=[jax.ShapeDtypeStruct(o, F32) for o in out...  2.94 us
    unnamed x14, local copies, waits for them, and re-layouts  2.63 us
  transfers between devices with their start and end apart: 14, of which 5 were waited for; matrix products, arithmetic and copies ran while one was open for 2% of the time, Pallas kernels for 8%

profile of v2, /device:TPU:0, one launch (start us, length us, event | category | flops | bytes accessed | tf_op | source)
XLA Modules:
  0.0 68.1 jit_solution(8060359926725462192)
XLA Ops:
  0.7 1.0 %copy-done.1 = bf16[128,2048]{1,0:T(8,128)(2,1)S(1)} copy-done((bf16[128,2048]{1,0:T(8,128)(2,1)S(1)}, bf16[128,2048]{1,0:T(8,128)(2,1)}, u32[]{:S(2)}) %copy-start.1) | copy-done | bytes 524312
  1.8 0.9 %copy-done.3 = bf16[300,128]{1,0:T(8,128)(2,1)S(1)} copy-done((bf16[300,128]{1,0:T(8,128)(2,1)S(1)}, bf16[300,128]{1,0:T(8,128)(2,1)}, u32[]{:S(2)}) %copy-start.3) | copy-done | bytes 76824
  2.7 0.7 %copy-done.5 = bf16[300,8]{0,1:T(8,128)(2,1)S(1)} copy-done((bf16[300,8]{0,1:T(8,128)(2,1)S(1)}, bf16[300,8]{0,1:T(8,128)(2,1)}, u32[]{:S(2)}) %copy-start.5) | copy-done | bytes 4824
  3.4 11.9 %front.1 = (f32[300,2048]{1,0:T(8,128)S(1)}, bf16[300,1024]{1,0:T(8,128)(2,1)S(1)}, f32[328,128]{1,0:T(8,128)S(1)}) custom-call(s32[3]{0:T(128)S(1)} %pad_add_fusion.pos_ref.refs_0_, bf16[300,128]{1,0:T(8,128)(2,1)S(1)} %copy-done.3, bf16[8,300]{1,0:T(8,128)(2,1)S(1)} %bitcast.7, bf16[1024,4096]{1,0:T(8,128)(2,1)} %bitcast.9, bf16[300,4096]{1,0:T(8,128)(2,1)} %ctx_ref.3, ...), custom_call_target="tpu_custom_call" | custom-call | flops 4880793600 | bytes 10846208 | tf_op jit(solution)/shard_map/front/pallas_call | solution.py:143
  15.3 2.1 %collective-permute-start.1 = (f32[328,128]{1,0:T(8,128)S(1)}, f32[328,128]{1,0:T(8,128)S(1)}, u32[]{:S(2)}, u32[]{:S(2)}) collective-permute-start(f32[328,128]{1,0:T(8,128)S(1)} %get-tuple-element.22.after_ref), channel_id=1, source_target_pairs={{0,1},{1,0},{2,3},{3,2},{4,5},{5,4},{6,7},{7,6},{8,9},{9,8},{10,11... | collective-permute-start | bytes 503816 | tf_op jit(solution)/shard_map/ppermute | solution.py:321
  17.4 5.5 %own_half.1.refs_1_ = f32[300,2048]{1,0:T(8,128)S(1)} custom-call(s32[3]{0:T(128)S(1)} %pad_add_fusion.pos_ref.refs_0_, bf16[300,128]{1,0:T(8,128)(2,1)S(1)} %copy-done.4, bf16[8,300]{1,0:T(8,128)(2,1)S(1)} %bitcast.8, bf16[300,1024]{1,0:T(8,128)(2,1)S(1)} %get-tuple-element.21.a_ref, bf16[1024,4096]{1,0:T(8,128)(2,1)} %bitcast.10, ...), custom_call_target="tpu_custom_call" | custom-call | flops 99778560000 | bytes 394035200 | tf_op jit(solution)/shard_map/own_half/pallas_call | solution.py:203
  22.9 0.8 %first_sum.1 = (f32[160,512]{1,0:T(8,128)S(1)}, f32[160,512]{1,0:T(8,128)S(1)}, f32[160,512]{1,0:T(8,128)S(1)}, f32[140,1024]{1,0:T(8,128)S(1)}, f32[160,512]{1,0:T(8,128)S(1)}, /*index=5*/f32[140,1024]{1,0:T(8,128)S(1)}) custom-call(s32[3]{0:T(128)S(1)} %pad_add_fusion.pos_ref.refs_0_, f32[300,2048]{1,0:T(8,128)S(1)} %own_half.1.refs_1_, ...), custom_call_target="tpu_custom_call" | custom-call | flops 1024 | bytes 1024 | tf_op jit(solution)/shard_map/first_sum/pallas_call | solution.py:228
  23.8 1.6 %collective-permute-start.2 = (f32[160,512]{1,0:T(8,128)S(1)}, f32[160,512]{1,0:T(8,128)S(1)}, u32[]{:S(2)}, u32[]{:S(2)}) collective-permute-start(f32[160,512]{1,0:T(8,128)S(1)} %get-tuple-element.25), channel_id=1, source_target_pairs={{0,16},{8,24},{16,32},{24,40},{32,48},{40,56},{48,0},{56,8},{1,17}... | collective-permute-start | bytes 983048 | tf_op jit(solution)/shard_map/ppermute | solution.py:321
  25.3 3.6 %collective-permute-start.6 = (f32[328,128]{1,0:T(8,128)S(1)}, f32[328,128]{1,0:T(8,128)S(1)}, u32[]{:S(2)}, u32[]{:S(2)}) collective-permute-start(f32[328,128]{1,0:T(8,128)S(1)} %add.15.refs_3_), channel_id=1, source_target_pairs={{0,2},{1,3},{2,0},{3,1},{4,6},{5,7},{6,4},{7,5},{8,10},{9,11},{10,... | collective-permute-start | bytes 503816 | tf_op jit(solution)/shard_map/ppermute | solution.py:321
  28.9 1.6 %collective-permute-start.5 = (f32[140,1024]{1,0:T(8,128)S(1)}, f32[140,1024]{1,0:T(8,128)S(1)}, u32[]{:S(2)}, u32[]{:S(2)}) collective-permute-start(f32[140,1024]{1,0:T(8,128)S(1)} %get-tuple-element.29), channel_id=1, source_target_pairs={{0,8},{8,0},{16,24},{24,16},{32,40},{40,32},{48,56},{56,48},{1,9},... | collective-permute-start | bytes 1720328 | tf_op jit(solution)/shard_map/ppermute | solution.py:321
  30.5 2.8 %collective-permute-start.3 = (f32[160,512]{1,0:T(8,128)S(1)}, f32[160,512]{1,0:T(8,128)S(1)}, u32[]{:S(2)}, u32[]{:S(2)}) collective-permute-start(f32[160,512]{1,0:T(8,128)S(1)} %get-tuple-element.26), channel_id=1, source_target_pairs={{0,32},{8,40},{16,48},{24,56},{32,0},{40,8},{48,16},{56,24},{1,33}... | collective-permute-start | bytes 983048 | tf_op jit(solution)/shard_map/ppermute | solution.py:321
  33.2 1.4 %collective-permute-start.4 = (f32[160,512]{1,0:T(8,128)S(1)}, f32[160,512]{1,0:T(8,128)S(1)}, u32[]{:S(2)}, u32[]{:S(2)}) collective-permute-start(f32[160,512]{1,0:T(8,128)S(1)} %get-tuple-element.27), channel_id=1, source_target_pairs={{0,48},{8,56},{16,0},{24,8},{32,16},{40,24},{48,32},{56,40},{1,49}... | collective-permute-start | bytes 983048 | tf_op jit(solution)/shard_map/ppermute | solution.py:321
  35.1 0.5 slice.8
  35.7 0.7 add_select_fusion
  36.3 3.3 %collective-permute-start.7 = (f32[328,128]{1,0:T(8,128)S(1)}, f32[328,128]{1,0:T(8,128)S(1)}, u32[]{:S(2)}, u32[]{:S(2)}) collective-permute-start(f32[328,128]{1,0:T(8,128)S(1)} %add_select_fusion), channel_id=1, source_target_pairs={{0,4},{1,5},{2,6},{3,7},{4,0},{5,1},{6,2},{7,3},{8,12},{9,13},{10,... | collective-permute-start | bytes 503816 | tf_op jit(solution)/shard_map/ppermute | solution.py:321
  39.6 10.5 %collective-permute-done.7 = f32[328,128]{1,0:T(8,128)S(1)} collective-permute-done((f32[328,128]{1,0:T(8,128)S(1)}, f32[328,128]{1,0:T(8,128)S(1)}, u32[]{:S(2)}, u32[]{:S(2)}) %collective-permute-start.7) | collective-permute-done | bytes 167968 | tf_op jit(solution)/shard_map/ppermute | solution.py:321
  50.4 3.5 %collective-permute-done.8.refs_8_ = f32[24,128]{1,0:T(8,128)S(1)} collective-permute-done((f32[24,128]{1,0:T(8,128)S(1)}, f32[24,128]{1,0:T(8,128)S(1)}, u32[]{:S(2)}, u32[]{:S(2)}) %collective-permute-start.8) | collective-permute-done | bytes 12320 | tf_op jit(solution)/shard_map/ppermute | solution.py:321
  54.0 0.7 %middle_sum.1 = (f32[160,256]{1,0:T(8,128)S(1)}, f32[160,256]{1,0:T(8,128)S(1)}, f32[168,256]{1,0:T(8,128)S(1)}, f32[168,256]{1,0:T(8,128)S(1)}, f32[168,256]{1,0:T(8,128)S(1)}, /*index=5*/f32[168,256]{1,0:T(8,128)S(1)}) custom-call(s32[3]{0:T(128)S(1)} %pad_add_fusion.pos_ref.refs_0_, f32[160,512]{1,0:T(8,128)S(1)} %get-tuple-element.24.refs_1_, ...), custom_call_target="tpu_custom_call" | custom-call | flops 1024 | bytes 1024 | tf_op jit(solution)/shard_map/middle_sum/pallas_call | solution.py:228
  54.7 1.5 %collective-permute-start.10 = (f32[168,256]{1,0:T(8,128)S(1)}, f32[168,256]{1,0:T(8,128)S(1)}, u32[]{:S(2)}, u32[]{:S(2)}) collective-permute-start(f32[168,256]{1,0:T(8,128)S(1)} %get-tuple-element.33), channel_id=1, source_target_pairs={{0,16},{8,24},{16,32},{24,40},{32,48},{40,56},{48,0},{56,8},{1,17}... | collective-permute-start | bytes 516104 | tf_op jit(solution)/shard_map/ppermute | solution.py:321
  56.2 1.7 %collective-permute-start.11 = (f32[168,256]{1,0:T(8,128)S(1)}, f32[168,256]{1,0:T(8,128)S(1)}, u32[]{:S(2)}, u32[]{:S(2)}) collective-permute-start(f32[168,256]{1,0:T(8,128)S(1)} %get-tuple-element.34), channel_id=1, source_target_pairs={{0,32},{8,40},{16,48},{24,56},{32,0},{40,8},{48,16},{56,24},{1,33}... | collective-permute-start | bytes 516104 | tf_op jit(solution)/shard_map/ppermute | solution.py:321
  57.9 2.2 %collective-permute-start.12 = (f32[168,256]{1,0:T(8,128)S(1)}, f32[168,256]{1,0:T(8,128)S(1)}, u32[]{:S(2)}, u32[]{:S(2)}) collective-permute-start(f32[168,256]{1,0:T(8,128)S(1)} %get-tuple-element.35), channel_id=1, source_target_pairs={{0,48},{8,56},{16,0},{24,8},{32,16},{40,24},{48,32},{56,40},{1,49}... | collective-permute-start | bytes 516104 | tf_op jit(solution)/shard_map/ppermute | solution.py:321
  60.3 1.3 %collective-permute-done.13.refs_8_ = f32[328,128]{1,0:T(8,128)S(1)} collective-permute-done((f32[328,128]{1,0:T(8,128)S(1)}, f32[328,128]{1,0:T(8,128)S(1)}, u32[]{:S(2)}, u32[]{:S(2)}) %collective-permute-start.13) | collective-permute-done | bytes 167968 | tf_op jit(solution)/shard_map/ppermute | solution.py:321
  61.5 5.2 %collective-permute-done.9.refs_2_ = f32[160,256]{1,0:T(8,128)S(1)} collective-permute-done((f32[160,256]{1,0:T(8,128)S(1)}, f32[160,256]{1,0:T(8,128)S(1)}, u32[]{:S(2)}, u32[]{:S(2)}) %collective-permute-start.9) | collective-permute-done | bytes 163872 | tf_op jit(solution)/shard_map/ppermute | solution.py:321
  66.7 1.4 %last_sum.1 = (f32[300,256]{1,0:T(8,128)}, f32[300,128]{1,0:T(8,128)}, f32[8,300]{1,0:T(8,128)}) custom-call(s32[3]{0:T(128)S(1)} %pad_add_fusion.pos_ref.refs_0_, f32[160,256]{1,0:T(8,128)S(1)} %get-tuple-element.30.refs_1_, f32[160,256]{1,0:T(8,128)S(1)} %collective-permute-done.9.refs_2_, f32[168,256]{1,0:T(8,128)S(1)} %get-tuple-element.32.refs_3_, ...), custom_call_target="tpu_custom_call" | custom-call | flops 1024 | bytes 1024 | tf_op jit(solution)/shard_map/last_sum/pallas_call | solution.py:228
  (29 shorter events, 1.0 us)
Async XLA Ops:
  0.7 1.0 %copy-start.1 = (bf16[128,2048]{1,0:T(8,128)(2,1)S(1)}, bf16[128,2048]{1,0:T(8,128)(2,1)}, u32[]{:S(2)}) copy-start(bf16[128,2048]{1,0:T(8,128)(2,1)} %mat_ref.3) | copy-start | bytes 1572868
  1.8 0.9 %copy-start.3 = (bf16[300,128]{1,0:T(8,128)(2,1)S(1)}, bf16[300,128]{1,0:T(8,128)(2,1)}, u32[]{:S(2)}) copy-start(bf16[300,128]{1,0:T(8,128)(2,1)} %word_ref.3) | copy-start | bytes 230404
  2.7 0.7 %copy-start.5 = (bf16[300,8]{0,1:T(8,128)(2,1)S(1)}, bf16[300,8]{0,1:T(8,128)(2,1)}, u32[]{:S(2)}) copy-start(bf16[300,8]{0,1:T(8,128)(2,1)} %param.9) | copy-start | bytes 14404
  3.3 14.0 %copy-start = (bf16[300,4096]{1,0:T(8,128)(2,1)S(1)}, bf16[300,4096]{1,0:T(8,128)(2,1)}, u32[]{:S(2)}) copy-start(bf16[300,4096]{1,0:T(8,128)(2,1)} %ctx_ref.3) | copy-start | bytes 7372804
  3.4 14.0 %copy-start.2 = (bf16[128,2048]{1,0:T(8,128)(2,1)S(1)}, bf16[128,2048]{1,0:T(8,128)(2,1)}, u32[]{:S(2)}) copy-start(bf16[128,2048]{1,0:T(8,128)(2,1)} %mat_ref.3) | copy-start | bytes 1572868
  3.4 14.0 %copy-start.4 = (bf16[300,128]{1,0:T(8,128)(2,1)S(1)}, bf16[300,128]{1,0:T(8,128)(2,1)}, u32[]{:S(2)}) copy-start(bf16[300,128]{1,0:T(8,128)(2,1)} %word_ref.3) | copy-start | bytes 230404
  3.4 14.0 %copy-start.6 = (bf16[300,8]{0,1:T(8,128)(2,1)S(1)}, bf16[300,8]{0,1:T(8,128)(2,1)}, u32[]{:S(2)}) copy-start(bf16[300,8]{0,1:T(8,128)(2,1)} %param.9) | copy-start | bytes 14404
  15.3 7.6 %collective-permute-start.1 = (f32[328,128]{1,0:T(8,128)S(1)}, f32[328,128]{1,0:T(8,128)S(1)}, u32[]{:S(2)}, u32[]{:S(2)}) collective-permute-start(f32[328,128]{1,0:T(8,128)S(1)} %get-tuple-element.22.after_ref), channel_id=1, source_target_pairs={{0,1},{1,0},{2,3},{3,2},{4,5},{5,4},{6,7},{7,6},{8,9},{9,8},{10,11... | collective-permute-start | bytes 503816 | tf_op jit(solution)/shard_map/ppermute | solution.py:321
  17.3 5.6 %collective-permute-start = (f32[300,2048]{1,0:T(8,128)S(1)}, f32[300,2048]{1,0:T(8,128)S(1)}, u32[]{:S(2)}, u32[]{:S(2)}) collective-permute-start(f32[300,2048]{1,0:T(8,128)S(1)} %get-tuple-element.23), channel_id=1, source_target_pairs={{0,64},{64,0},{1,65},{65,1},{2,66},{66,2},{3,67},{67,3},{4,68},{68... | collective-permute-start | bytes 7372808 | tf_op jit(solution)/shard_map/ppermute | solution.py:321
  23.8 11.4 %collective-permute-start.2 = (f32[160,512]{1,0:T(8,128)S(1)}, f32[160,512]{1,0:T(8,128)S(1)}, u32[]{:S(2)}, u32[]{:S(2)}) collective-permute-start(f32[160,512]{1,0:T(8,128)S(1)} %get-tuple-element.25), channel_id=1, source_target_pairs={{0,16},{8,24},{16,32},{24,40},{32,48},{40,56},{48,0},{56,8},{1,17}... | collective-permute-start | bytes 983048 | tf_op jit(solution)/shard_map/ppermute | solution.py:321
  25.3 10.3 %collective-permute-start.6 = (f32[328,128]{1,0:T(8,128)S(1)}, f32[328,128]{1,0:T(8,128)S(1)}, u32[]{:S(2)}, u32[]{:S(2)}) collective-permute-start(f32[328,128]{1,0:T(8,128)S(1)} %add.15.refs_3_), channel_id=1, source_target_pairs={{0,2},{1,3},{2,0},{3,1},{4,6},{5,7},{6,4},{7,5},{8,10},{9,11},{10,... | collective-permute-start | bytes 503816 | tf_op jit(solution)/shard_map/ppermute | solution.py:321
  28.9 25.0 %collective-permute-start.5 = (f32[140,1024]{1,0:T(8,128)S(1)}, f32[140,1024]{1,0:T(8,128)S(1)}, u32[]{:S(2)}, u32[]{:S(2)}) collective-permute-start(f32[140,1024]{1,0:T(8,128)S(1)} %get-tuple-element.29), channel_id=1, source_target_pairs={{0,8},{8,0},{16,24},{24,16},{32,40},{40,32},{48,56},{56,48},{1,9},... | collective-permute-start | bytes 1720328 | tf_op jit(solution)/shard_map/ppermute | solution.py:321
  30.5 19.9 %collective-permute-start.3 = (f32[160,512]{1,0:T(8,128)S(1)}, f32[160,512]{1,0:T(8,128)S(1)}, u32[]{:S(2)}, u32[]{:S(2)}) collective-permute-start(f32[160,512]{1,0:T(8,128)S(1)} %get-tuple-element.26), channel_id=1, source_target_pairs={{0,32},{8,40},{16,48},{24,56},{32,0},{40,8},{48,16},{56,24},{1,33}... | collective-permute-start | bytes 983048 | tf_op jit(solution)/shard_map/ppermute | solution.py:321
  33.2 17.2 %collective-permute-start.4 = (f32[160,512]{1,0:T(8,128)S(1)}, f32[160,512]{1,0:T(8,128)S(1)}, u32[]{:S(2)}, u32[]{:S(2)}) collective-permute-start(f32[160,512]{1,0:T(8,128)S(1)} %get-tuple-element.27), channel_id=1, source_target_pairs={{0,48},{8,56},{16,0},{24,8},{32,16},{40,24},{48,32},{56,40},{1,49}... | collective-permute-start | bytes 983048 | tf_op jit(solution)/shard_map/ppermute | solution.py:321
  36.3 13.8 %collective-permute-start.7 = (f32[328,128]{1,0:T(8,128)S(1)}, f32[328,128]{1,0:T(8,128)S(1)}, u32[]{:S(2)}, u32[]{:S(2)}) collective-permute-start(f32[328,128]{1,0:T(8,128)S(1)} %add_select_fusion), channel_id=1, source_target_pairs={{0,4},{1,5},{2,6},{3,7},{4,0},{5,1},{6,2},{7,3},{8,12},{9,13},{10,... | collective-permute-start | bytes 503816 | tf_op jit(solution)/shard_map/ppermute | solution.py:321
  50.2 3.8 %collective-permute-start.8 = (f32[24,128]{1,0:T(8,128)S(1)}, f32[24,128]{1,0:T(8,128)S(1)}, u32[]{:S(2)}, u32[]{:S(2)}) collective-permute-start(f32[24,128]{1,0:T(8,128)S(1)} %slice.9.refs_7_), channel_id=1, source_target_pairs={{0,8},{8,0},{16,24},{24,16},{32,40},{40,32},{48,56},{56,48},{1,9},... | collective-permute-start | bytes 36872 | tf_op jit(solution)/shard_map/ppermute | solution.py:321
  54.7 12.1 %collective-permute-start.10 = (f32[168,256]{1,0:T(8,128)S(1)}, f32[168,256]{1,0:T(8,128)S(1)}, u32[]{:S(2)}, u32[]{:S(2)}) collective-permute-start(f32[168,256]{1,0:T(8,128)S(1)} %get-tuple-element.33), channel_id=1, source_target_pairs={{0,16},{8,24},{16,32},{24,40},{32,48},{40,56},{48,0},{56,8},{1,17}... | collective-permute-start | bytes 516104 | tf_op jit(solution)/shard_map/ppermute | solution.py:321
  56.2 10.5 %collective-permute-start.11 = (f32[168,256]{1,0:T(8,128)S(1)}, f32[168,256]{1,0:T(8,128)S(1)}, u32[]{:S(2)}, u32[]{:S(2)}) collective-permute-start(f32[168,256]{1,0:T(8,128)S(1)} %get-tuple-element.34), channel_id=1, source_target_pairs={{0,32},{8,40},{16,48},{24,56},{32,0},{40,8},{48,16},{56,24},{1,33}... | collective-permute-start | bytes 516104 | tf_op jit(solution)/shard_map/ppermute | solution.py:321
  57.9 8.8 %collective-permute-start.12 = (f32[168,256]{1,0:T(8,128)S(1)}, f32[168,256]{1,0:T(8,128)S(1)}, u32[]{:S(2)}, u32[]{:S(2)}) collective-permute-start(f32[168,256]{1,0:T(8,128)S(1)} %get-tuple-element.35), channel_id=1, source_target_pairs={{0,48},{8,56},{16,0},{24,8},{32,16},{40,24},{48,32},{56,40},{1,49}... | collective-permute-start | bytes 516104 | tf_op jit(solution)/shard_map/ppermute | solution.py:321
  60.1 1.4 %collective-permute-start.13 = (f32[328,128]{1,0:T(8,128)S(1)}, f32[328,128]{1,0:T(8,128)S(1)}, u32[]{:S(2)}, u32[]{:S(2)}) collective-permute-start(f32[328,128]{1,0:T(8,128)S(1)} %add.17.refs_7_), channel_id=1, source_target_pairs={{0,64},{64,0},{1,65},{65,1},{2,66},{66,2},{3,67},{67,3},{4,68},{68... | collective-permute-start | bytes 503816 | tf_op jit(solution)/shard_map/ppermute | solution.py:321
  60.1 6.6 %collective-permute-start.9 = (f32[160,256]{1,0:T(8,128)S(1)}, f32[160,256]{1,0:T(8,128)S(1)}, u32[]{:S(2)}, u32[]{:S(2)}) collective-permute-start(f32[160,256]{1,0:T(8,128)S(1)} %get-tuple-element.31), channel_id=1, source_target_pairs={{0,8},{8,0},{16,24},{24,16},{32,40},{40,32},{48,56},{56,48},{1,9},... | collective-permute-start | bytes 491528 | tf_op jit(solution)/shard_map/ppermute | solution.py:321

commit v3 on v2

--- a/solution.py
+++ b/solution.py
@@ -14,8 +14,8 @@
 BIG = 50 * MIB
 OWN = 42 * MIB
 WORD = 50 * MIB
-FRONT_TILE = 512
-TOP = 160
+FRONT_TILE = 1024
+TOP = 128
 NT = (((1,), (1,)), ((), ()))
 TN = (((0,), (0,)), ((), ()))
 
@@ -35,6 +35,21 @@
 def split_two(v):
     hi = v.astype(BF16)
     return hi, (v - hi.astype(F32)).astype(BF16)
+
+
+def split_diagonal(v):
+    n = v.shape[0]
+    hi = v.astype(BF16)
+    row = lax.broadcasted_iota(jnp.int32, (n, n), 0)
+    col = lax.broadcasted_iota(jnp.int32, (n, n), 1)
+    rest = jnp.where(row == col, v - hi.astype(F32), 0.0)
+    return hi, jnp.sum(rest, axis=1, keepdims=True)
+
+
+def square(parts):
+    left, corner = parts
+    right = jnp.concatenate([left[left.shape[1] :].T, corner], axis=0)
+    return jnp.concatenate([left, right], axis=1)
 
 
 def chunk_count(rank):
@@ -92,26 +107,31 @@
     a_out[...] = a
     gram_w = dot_nt(w, w)
     gram_o = dot_tn(o, o)
-    m_hi, m_lo = split_two(gram_w * gram_o)
+    m_hi, m_rest = split_diagonal(gram_w * gram_o)
     b = m = own = other = None
 
     def plus(total, term):
-        return term if total is None else total + term
+        if total is None:
+            return term
+        if isinstance(term, tuple):
+            return tuple(t + u for t, u in zip(total, term))
+        return total + term
 
     for i in range(steps):
         for c in loads[i]:
             c.wait()
         c = c_buf[i]
-        gram = dot_nt(c, c)
+        gram = (dot_nt(c, c[:256]), dot_nt(c[256:], c[256:]))
         if i < half:
-            ctx_out[:, pl.ds(i * tile, tile)] = dot(m_hi, c) + dot(m_lo, c) - dot(a, d_buf[i])
+            ctx_out[:, pl.ds(i * tile, tile)] = dot(m_hi, c) - dot(a, d_buf[i]) + m_rest * c.astype(F32)
             other = plus(other, gram)
         else:
             m = plus(m, dot_nt(c, m_buf[i - half]))
             own = plus(own, gram)
         b = plus(b, dot_nt(c, d_buf[i]))
 
-    both = own + other
+    own = square(own)
+    both = own + square(other)
     n_hi, n_lo = split_two(gram_o * both + own)
     b_hi, b_lo = split_two(b * wide_o)
     total = dot(n_hi, w) + dot(n_lo, w) - m
@@ -183,11 +203,12 @@
     w = word_ref[...]
     o = off_ref[...]
     a = a_ref[...]
-    hi, lo = split_two(dot_nt(w, w) * (dot_tn(o, o) + 1.0))
+    hi, rest = split_diagonal(dot_nt(w, w) * (dot_tn(o, o) + 1.0))
     for i in range(steps):
         for c in loads[i]:
             c.wait()
-        total = dot(hi, c_buf[i]) + dot(lo, c_buf[i]) - dot(w, m_buf[i]) - dot(a, d_buf[i])
+        c = c_buf[i]
+        total = dot(hi, c) - dot(w, m_buf[i]) - dot(a, d_buf[i]) + rest * c.astype(F32)
         out_ref[:, pl.ds(i * tile, tile)] = total
 
 
@@ -240,7 +261,7 @@
     return pl.ds(pl.multiple_of(start, 128), width)
 
 
-def first_sum(pos_ref, own_ref, got_ref, x1_ref, x2_ref, x3_ref, y_ref, kx_ref, ky_ref):
+def first_sum(pos_ref, own_ref, got_ref, part_ref, more_ref, x1_ref, x2_ref, x3_ref, y_ref, kx_ref, ky_ref, sum_ref):
     x, y = pos_ref[1], pos_ref[2]
     top, width = kx_ref.shape
     low, span = ky_ref.shape
@@ -252,6 +273,7 @@
         for k in range(4):
             at = lanes((2 * k + side) * block, block)
             ref[:, pl.ds(k * block, block)] = own_ref[pl.ds(top, low), at] + got_ref[pl.ds(top, low), at]
+    sum_ref[...] = part_ref[...] + more_ref[...]
 
 
 def middle_sum(pos_ref, k_ref, a_ref, b_ref, c_ref, l_ref, g_ref, off_ref, more_ref, *refs):
@@ -334,29 +356,26 @@
     off_t = offset_factor.T
     other, a, part = front_part(pos, data, matrix_data, word_factor, off_t, context_factor)
     got = send(other, "section", SWAP)
-    z1 = send(part, "cols", Z_PAIR[0])
+    more = send(part, "cols", Y_HIGH)
     own = own_part(pos, data, matrix_data, word_factor, off_t, context_factor, a, part)
-    part = part + z1
-    z2 = send(part, "cols", Z_PAIR[1])
 
     top = TOP
     low = rank - top
     block = width // 16
     extra = chunk_count(rank) * offsets
-    x1, x2, x3, y1, kx, ky = whole_call(
-        first_sum, [(top, 2 * block)] * 3 + [(low, 4 * block), (top, 2 * block), (low, 4 * block)],
-        "first_sum", pos, own, got, after=(part,),
+    x1, x2, x3, y1, kx, ky, part = whole_call(
+        first_sum, [(top, 2 * block)] * 3 + [(low, 4 * block), (top, 2 * block), (low, 4 * block), part.shape],
+        "first_sum", pos, own, got, part, more,
     )
     f1 = send(x1, "rows", X_HOP[1])
     f3 = send(x3, "rows", X_HOP[3])
     g = send(y1, "rows", Y_LOW)
     f2 = send(x2, "rows", X_HOP[2])
-    never = row < 0
-    part = part + z2
-    part = jnp.where(never, f1[:1, :1], part)
-    word = part + send(part, "cols", Y_HIGH)
+    part = part + send(part, "cols", Z_PAIR[0])
+    word = part + send(part, "cols", Z_PAIR[1])
     off = word[word.shape[0] - extra :]
     more = send(off, "rows", Y_LOW)
+    other_word = send(word, "section", SWAP)
     longer = (-(-low // 8) * 8 + extra, block)
     sx, kx, x1, x2, x3, ky = whole_call(
         middle_sum, [(top, block)] * 2 + [longer] * 4, "middle_sum", pos, kx, f1, f2, f3, ky, g, off, more
@@ -365,7 +384,6 @@
     f3 = send(x3, "rows", X_HOP[3])
     f2 = send(x2, "rows", X_HOP[2])
     g = send(sx, "rows", Y_LOW)
-    other_word = send(word, "section", SWAP)
     scales = (
         1.0 / math.sqrt(all_words * all_offsets),
         1.0 / math.sqrt(all_contexts * all_offsets),

time: 69 us -> 57.4 us (0.83)
  waiting for transfers between devices: 21 us -> 12.1 us
  Pallas kernels: 20.3 us -> 18.1 us
  starting transfers between devices: 22.1 us -> 23.4 us
    ppermute x14, waiting for transfers between devices: 21 us -> 12.1 us  [send(): return lax.ppermute(v, axis, perm)]
    pallas_call x1, Pallas kernels: 11.9 us -> 10.2 us  [front_part(): pl.pallas_call(front_kernel, out_shape=[jax.ShapeDtypeStruct((rank, width...]
    ppermute x14, starting transfers between devices: 22.1 us -> 23.4 us  [send(): return lax.ppermute(v, axis, perm)]
  transfers between devices with their start and end apart: 14 -> 14, of which waited for: 5 -> 6; matrix products, arithmetic and copies ran while one was open for 2% -> 0% of each run, Pallas kernels for 8% -> 9%
where the time goes in v3:
time: 57.4 us; the launch traced here: 57.2 us
  starting transfers between devices  23.4 us (41%)
  Pallas kernels  18.1 us (32%)
  waiting for transfers between devices  12.1 us (21%)
  local copies, waits for them, and re-layouts  2.64 us (5%)
  between operations  0.75 us (1%)
    ppermute x14, starting transfers between devices, send(): return lax.ppermute(v, axis, perm)  23.4 us
    ppermute x14, waiting for transfers between devices, send(): return lax.ppermute(v, axis, perm)  12.1 us
    pallas_call x1, Pallas kernels, front_part(): pl.pallas_call(front_kernel, out_shape=[jax.ShapeDtypeStruct((rank, width...  10.2 us
    pallas_call x1, Pallas kernels, own_part(): pl.pallas_call(own_kernel, out_shape=jax.ShapeDtypeStruct((rank, half), F...  4.94 us
    pallas_call x3, Pallas kernels, whole_call(): pl.pallas_call(body, out_shape=[jax.ShapeDtypeStruct(o, F32) for o in out...  2.98 us
    unnamed x14, local copies, waits for them, and re-layouts  2.63 us
  transfers between devices with their start and end apart: 14, of which 6 were waited for; matrix products, arithmetic and copies ran while one was open for 0% of the time, Pallas kernels for 9%

profile of v3, /device:TPU:0, one launch (start us, length us, event | category | flops | bytes accessed | tf_op | source)
XLA Modules:
  0.0 57.2 jit_solution(16118801467089417573)
XLA Ops:
  0.7 1.0 %copy-done.1 = bf16[128,2048]{1,0:T(8,128)(2,1)S(1)} copy-done((bf16[128,2048]{1,0:T(8,128)(2,1)S(1)}, bf16[128,2048]{1,0:T(8,128)(2,1)}, u32[]{:S(2)}) %copy-start.1) | copy-done | bytes 524312
  1.8 0.9 %copy-done.3 = bf16[300,128]{1,0:T(8,128)(2,1)S(1)} copy-done((bf16[300,128]{1,0:T(8,128)(2,1)S(1)}, bf16[300,128]{1,0:T(8,128)(2,1)}, u32[]{:S(2)}) %copy-start.3) | copy-done | bytes 76824
  3.4 10.2 %front.1 = (f32[300,2048]{1,0:T(8,128)S(1)}, bf16[300,1024]{1,0:T(8,128)(2,1)S(1)}, f32[328,128]{1,0:T(8,128)S(1)}) custom-call(s32[3]{0:T(128)S(1)} %pad_add_fusion.pos_ref.refs_0_, bf16[300,128]{1,0:T(8,128)(2,1)S(1)} %copy-done.3, bf16[8,300]{1,0:T(8,128)(2,1)S(1)} %bitcast.6, bf16[1024,4096]{1,0:T(8,128)(2,1)} %bitcast.8, bf16[300,4096]{1,0:T(8,128)(2,1)} %ctx_ref.3, ...), custom_call_target="tpu_custom_call" | custom-call | flops 4880793600 | bytes 10846208 | tf_op jit(solution)/shard_map/front/pallas_call | solution.py:163
  13.6 3.4 %collective-permute-start.1 = (f32[328,128]{1,0:T(8,128)S(1)}, f32[328,128]{1,0:T(8,128)S(1)}, u32[]{:S(2)}, u32[]{:S(2)}) collective-permute-start(f32[328,128]{1,0:T(8,128)S(1)} %get-tuple-element.23.after_ref.refs_3_), channel_id=1, source_target_pairs={{0,4},{1,5},{2,6},{3,7},{4,0},{5,1},{6,2},{7,3},{8,12},{9,13},{10,... | collective-permute-start | bytes 503816 | tf_op jit(solution)/shard_map/ppermute | solution.py:343
  17.0 4.9 %own_half.1.refs_1_ = f32[300,2048]{1,0:T(8,128)S(1)} custom-call(s32[3]{0:T(128)S(1)} %pad_add_fusion.pos_ref.refs_0_, bf16[300,128]{1,0:T(8,128)(2,1)S(1)} %copy-done.4, bf16[8,300]{1,0:T(8,128)(2,1)S(1)} %bitcast.7, bf16[300,1024]{1,0:T(8,128)(2,1)S(1)} %get-tuple-element.22.a_ref, bf16[1024,4096]{1,0:T(8,128)(2,1)} %bitcast.9, ...), custom_call_target="tpu_custom_call" | custom-call | flops 99778560000 | bytes 394035200 | tf_op jit(solution)/shard_map/own_half/pallas_call | solution.py:224
  21.9 0.9 %first_sum.1 = (f32[128,512]{1,0:T(8,128)S(1)}, f32[128,512]{1,0:T(8,128)S(1)}, f32[128,512]{1,0:T(8,128)S(1)}, f32[172,1024]{1,0:T(8,128)S(1)}, f32[128,512]{1,...) custom-call(s32[3]{0:T(128)S(1)} %pad_add_fusion.pos_ref.refs_0_, f32[300,2048]{1,0:T(8,128)S(1)} %own_half.1.refs_1_, ...), custom_call_target="tpu_custom_call" | custom-call | flops 1024 | bytes 1024 | tf_op jit(solution)/shard_map/first_sum/pallas_call | solution.py:249
  22.8 1.0 %collective-permute-start.5 = (f32[172,1024]{1,0:T(8,128)S(1)}, f32[172,1024]{1,0:T(8,128)S(1)}, u32[]{:S(2)}, u32[]{:S(2)}) collective-permute-start(f32[172,1024]{1,0:T(8,128)S(1)} %get-tuple-element.30), channel_id=1, source_target_pairs={{0,8},{8,0},{16,24},{24,16},{32,40},{40,32},{48,56},{56,48},{1,9},... | collective-permute-start | bytes 2113544 | tf_op jit(solution)/shard_map/ppermute | solution.py:343
  23.8 1.9 %collective-permute-start.6 = (f32[328,128]{1,0:T(8,128)S(1)}, f32[328,128]{1,0:T(8,128)S(1)}, u32[]{:S(2)}, u32[]{:S(2)}) collective-permute-start(f32[328,128]{1,0:T(8,128)S(1)} %get-tuple-element.31), channel_id=1, source_target_pairs={{0,1},{1,0},{2,3},{3,2},{4,5},{5,4},{6,7},{7,6},{8,9},{9,8},{10,11... | collective-permute-start | bytes 503816 | tf_op jit(solution)/shard_map/ppermute | solution.py:343
  25.7 1.5 %collective-permute-start.2 = (f32[128,512]{1,0:T(8,128)S(1)}, f32[128,512]{1,0:T(8,128)S(1)}, u32[]{:S(2)}, u32[]{:S(2)}) collective-permute-start(f32[128,512]{1,0:T(8,128)S(1)} %get-tuple-element.26), channel_id=1, source_target_pairs={{0,16},{8,24},{16,32},{24,40},{32,48},{40,56},{48,0},{56,8},{1,17}... | collective-permute-start | bytes 786440 | tf_op jit(solution)/shard_map/ppermute | solution.py:343
  27.2 2.7 %collective-permute-start.3 = (f32[128,512]{1,0:T(8,128)S(1)}, f32[128,512]{1,0:T(8,128)S(1)}, u32[]{:S(2)}, u32[]{:S(2)}) collective-permute-start(f32[128,512]{1,0:T(8,128)S(1)} %get-tuple-element.27), channel_id=1, source_target_pairs={{0,32},{8,40},{16,48},{24,56},{32,0},{40,8},{48,16},{56,24},{1,33}... | collective-permute-start | bytes 786440 | tf_op jit(solution)/shard_map/ppermute | solution.py:343
  29.9 1.4 %collective-permute-start.4 = (f32[128,512]{1,0:T(8,128)S(1)}, f32[128,512]{1,0:T(8,128)S(1)}, u32[]{:S(2)}, u32[]{:S(2)}) collective-permute-start(f32[128,512]{1,0:T(8,128)S(1)} %get-tuple-element.28), channel_id=1, source_target_pairs={{0,48},{8,56},{16,0},{24,8},{32,16},{40,24},{48,32},{56,40},{1,49}... | collective-permute-start | bytes 786440 | tf_op jit(solution)/shard_map/ppermute | solution.py:343
  31.4 3.7 %collective-permute-start.7 = (f32[328,128]{1,0:T(8,128)S(1)}, f32[328,128]{1,0:T(8,128)S(1)}, u32[]{:S(2)}, u32[]{:S(2)}) collective-permute-start(f32[328,128]{1,0:T(8,128)S(1)} %add.12), channel_id=1, source_target_pairs={{0,2},{1,3},{2,0},{3,1},{4,6},{5,7},{6,4},{7,5},{8,10},{9,11},{10,... | collective-permute-start | bytes 503816 | tf_op jit(solution)/shard_map/ppermute | solution.py:343
  35.1 3.3 %collective-permute-done.7 = f32[328,128]{1,0:T(8,128)S(1)} collective-permute-done((f32[328,128]{1,0:T(8,128)S(1)}, f32[328,128]{1,0:T(8,128)S(1)}, u32[]{:S(2)}, u32[]{:S(2)}) %collective-permute-start.7) | collective-permute-done | bytes 167968 | tf_op jit(solution)/shard_map/ppermute | solution.py:343
  38.4 1.4 %collective-permute-start.8 = (f32[24,128]{1,0:T(8,128)S(1)}, f32[24,128]{1,0:T(8,128)S(1)}, u32[]{:S(2)}, u32[]{:S(2)}) collective-permute-start(f32[24,128]{1,0:T(8,128)S(1)} %slice.4.refs_7_), channel_id=1, source_target_pairs={{0,8},{8,0},{16,24},{24,16},{32,40},{40,32},{48,56},{56,48},{1,9},... | collective-permute-start | bytes 36872 | tf_op jit(solution)/shard_map/ppermute | solution.py:343
  39.8 1.6 %collective-permute-done.3.refs_3_ = f32[128,512]{1,0:T(8,128)S(1)} collective-permute-done((f32[128,512]{1,0:T(8,128)S(1)}, f32[128,512]{1,0:T(8,128)S(1)}, u32[]{:S(2)}, u32[]{:S(2)}) %collective-permute-start.3) | collective-permute-done | bytes 262176 | tf_op jit(solution)/shard_map/ppermute | solution.py:343
  41.4 0.8 %collective-permute-done.8.refs_8_ = f32[24,128]{1,0:T(8,128)S(1)} collective-permute-done((f32[24,128]{1,0:T(8,128)S(1)}, f32[24,128]{1,0:T(8,128)S(1)}, u32[]{:S(2)}, u32[]{:S(2)}) %collective-permute-start.8) | collective-permute-done | bytes 12320 | tf_op jit(solution)/shard_map/ppermute | solution.py:343
  42.2 0.7 %middle_sum.1 = (f32[128,256]{1,0:T(8,128)S(1)}, f32[128,256]{1,0:T(8,128)S(1)}, f32[200,256]{1,0:T(8,128)S(1)}, f32[200,256]{1,0:T(8,128)S(1)}, f32[200,256]{1,0:T(8,128)S(1)}, /*index=5*/f32[200,256]{1,0:T(8,128)S(1)}) custom-call(s32[3]{0:T(128)S(1)} %pad_add_fusion.pos_ref.refs_0_, f32[128,512]{1,0:T(8,128)S(1)} %get-tuple-element.25.refs_1_, ...), custom_call_target="tpu_custom_call" | custom-call | flops 1024 | bytes 1024 | tf_op jit(solution)/shard_map/middle_sum/pallas_call | solution.py:249
  42.9 1.0 %collective-permute-start.10 = (f32[200,256]{1,0:T(8,128)S(1)}, f32[200,256]{1,0:T(8,128)S(1)}, u32[]{:S(2)}, u32[]{:S(2)}) collective-permute-start(f32[200,256]{1,0:T(8,128)S(1)} %get-tuple-element.35), channel_id=1, source_target_pairs={{0,16},{8,24},{16,32},{24,40},{32,48},{40,56},{48,0},{56,8},{1,17}... | collective-permute-start | bytes 614408 | tf_op jit(solution)/shard_map/ppermute | solution.py:343
  43.9 2.8 %collective-permute-start.11 = (f32[200,256]{1,0:T(8,128)S(1)}, f32[200,256]{1,0:T(8,128)S(1)}, u32[]{:S(2)}, u32[]{:S(2)}) collective-permute-start(f32[200,256]{1,0:T(8,128)S(1)} %get-tuple-element.36), channel_id=1, source_target_pairs={{0,32},{8,40},{16,48},{24,56},{32,0},{40,8},{48,16},{56,24},{1,33}... | collective-permute-start | bytes 614408 | tf_op jit(solution)/shard_map/ppermute | solution.py:343
  46.7 1.4 %collective-permute-start.12 = (f32[200,256]{1,0:T(8,128)S(1)}, f32[200,256]{1,0:T(8,128)S(1)}, u32[]{:S(2)}, u32[]{:S(2)}) collective-permute-start(f32[200,256]{1,0:T(8,128)S(1)} %get-tuple-element.37), channel_id=1, source_target_pairs={{0,48},{8,56},{16,0},{24,8},{32,16},{40,24},{48,32},{56,40},{1,49}... | collective-permute-start | bytes 614408 | tf_op jit(solution)/shard_map/ppermute | solution.py:343
  48.1 1.3 %collective-permute-start.9 = (f32[128,256]{1,0:T(8,128)S(1)}, f32[128,256]{1,0:T(8,128)S(1)}, u32[]{:S(2)}, u32[]{:S(2)}) collective-permute-start(f32[128,256]{1,0:T(8,128)S(1)} %get-tuple-element.33), channel_id=1, source_target_pairs={{0,8},{8,0},{16,24},{24,16},{32,40},{40,32},{48,56},{56,48},{1,9},... | collective-permute-start | bytes 393224 | tf_op jit(solution)/shard_map/ppermute | solution.py:343
  49.5 4.5 %collective-permute-done.9.refs_2_ = f32[128,256]{1,0:T(8,128)S(1)} collective-permute-done((f32[128,256]{1,0:T(8,128)S(1)}, f32[128,256]{1,0:T(8,128)S(1)}, u32[]{:S(2)}, u32[]{:S(2)}) %collective-permute-start.9) | collective-permute-done | bytes 131104 | tf_op jit(solution)/shard_map/ppermute | solution.py:343
  54.1 1.7 %collective-permute-done.11.refs_5_ = f32[200,256]{1,0:T(8,128)S(1)} collective-permute-done((f32[200,256]{1,0:T(8,128)S(1)}, f32[200,256]{1,0:T(8,128)S(1)}, u32[]{:S(2)}, u32[]{:S(2)}) %collective-permute-start.11) | collective-permute-done | bytes 204832 | tf_op jit(solution)/shard_map/ppermute | solution.py:343
  55.8 1.4 %last_sum.1 = (f32[300,256]{1,0:T(8,128)}, f32[300,128]{1,0:T(8,128)}, f32[8,300]{1,0:T(8,128)}) custom-call(s32[3]{0:T(128)S(1)} %pad_add_fusion.pos_ref.refs_0_, f32[128,256]{1,0:T(8,128)S(1)} %get-tuple-element.32.refs_1_, f32[128,256]{1,0:T(8,128)S(1)} %collective-permute-done.9.refs_2_, f32[200,256]{1,0:T(8,128)S(1)} %get-tuple-element.34.refs_3_, ...), custom_call_target="tpu_custom_call" | custom-call | flops 1024 | bytes 1024 | tf_op jit(solution)/shard_map/last_sum/pallas_call | solution.py:249
  (27 shorter events, 1.0 us)
Async XLA Ops:
  0.7 1.0 %copy-start.1 = (bf16[128,2048]{1,0:T(8,128)(2,1)S(1)}, bf16[128,2048]{1,0:T(8,128)(2,1)}, u32[]{:S(2)}) copy-start(bf16[128,2048]{1,0:T(8,128)(2,1)} %mat_ref.3) | copy-start | bytes 1572868
  1.8 0.9 %copy-start.3 = (bf16[300,128]{1,0:T(8,128)(2,1)S(1)}, bf16[300,128]{1,0:T(8,128)(2,1)}, u32[]{:S(2)}) copy-start(bf16[300,128]{1,0:T(8,128)(2,1)} %word_ref.3) | copy-start | bytes 230404
  2.7 0.7 %copy-start.5 = (bf16[300,8]{0,1:T(8,128)(2,1)S(1)}, bf16[300,8]{0,1:T(8,128)(2,1)}, u32[]{:S(2)}) copy-start(bf16[300,8]{0,1:T(8,128)(2,1)} %param.9) | copy-start | bytes 14404
  3.3 13.6 %copy-start = (bf16[300,4096]{1,0:T(8,128)(2,1)S(1)}, bf16[300,4096]{1,0:T(8,128)(2,1)}, u32[]{:S(2)}) copy-start(bf16[300,4096]{1,0:T(8,128)(2,1)} %ctx_ref.3) | copy-start | bytes 7372804
  3.4 13.6 %copy-start.2 = (bf16[128,2048]{1,0:T(8,128)(2,1)S(1)}, bf16[128,2048]{1,0:T(8,128)(2,1)}, u32[]{:S(2)}) copy-start(bf16[128,2048]{1,0:T(8,128)(2,1)} %mat_ref.3) | copy-start | bytes 1572868
  3.4 13.6 %copy-start.4 = (bf16[300,128]{1,0:T(8,128)(2,1)S(1)}, bf16[300,128]{1,0:T(8,128)(2,1)}, u32[]{:S(2)}) copy-start(bf16[300,128]{1,0:T(8,128)(2,1)} %word_ref.3) | copy-start | bytes 230404
  3.4 13.6 %copy-start.6 = (bf16[300,8]{0,1:T(8,128)(2,1)S(1)}, bf16[300,8]{0,1:T(8,128)(2,1)}, u32[]{:S(2)}) copy-start(bf16[300,8]{0,1:T(8,128)(2,1)} %param.9) | copy-start | bytes 14404
  13.6 8.3 %collective-permute-start.1 = (f32[328,128]{1,0:T(8,128)S(1)}, f32[328,128]{1,0:T(8,128)S(1)}, u32[]{:S(2)}, u32[]{:S(2)}) collective-permute-start(f32[328,128]{1,0:T(8,128)S(1)} %get-tuple-element.23.after_ref.refs_3_), channel_id=1, source_target_pairs={{0,4},{1,5},{2,6},{3,7},{4,0},{5,1},{6,2},{7,3},{8,12},{9,13},{10,... | collective-permute-start | bytes 503816 | tf_op jit(solution)/shard_map/ppermute | solution.py:343
  16.9 5.0 %collective-permute-start = (f32[300,2048]{1,0:T(8,128)S(1)}, f32[300,2048]{1,0:T(8,128)S(1)}, u32[]{:S(2)}, u32[]{:S(2)}) collective-permute-start(f32[300,2048]{1,0:T(8,128)S(1)} %get-tuple-element.24), channel_id=1, source_target_pairs={{0,64},{64,0},{1,65},{65,1},{2,66},{66,2},{3,67},{67,3},{4,68},{68... | collective-permute-start | bytes 7372808 | tf_op jit(solution)/shard_map/ppermute | solution.py:343
  22.8 19.4 %collective-permute-start.5 = (f32[172,1024]{1,0:T(8,128)S(1)}, f32[172,1024]{1,0:T(8,128)S(1)}, u32[]{:S(2)}, u32[]{:S(2)}) collective-permute-start(f32[172,1024]{1,0:T(8,128)S(1)} %get-tuple-element.30), channel_id=1, source_target_pairs={{0,8},{8,0},{16,24},{24,16},{32,40},{40,32},{48,56},{56,48},{1,9},... | collective-permute-start | bytes 2113544 | tf_op jit(solution)/shard_map/ppermute | solution.py:343
  23.8 7.6 %collective-permute-start.6 = (f32[328,128]{1,0:T(8,128)S(1)}, f32[328,128]{1,0:T(8,128)S(1)}, u32[]{:S(2)}, u32[]{:S(2)}) collective-permute-start(f32[328,128]{1,0:T(8,128)S(1)} %get-tuple-element.31), channel_id=1, source_target_pairs={{0,1},{1,0},{2,3},{3,2},{4,5},{5,4},{6,7},{7,6},{8,9},{9,8},{10,11... | collective-permute-start | bytes 503816 | tf_op jit(solution)/shard_map/ppermute | solution.py:343
  25.7 14.1 %collective-permute-start.2 = (f32[128,512]{1,0:T(8,128)S(1)}, f32[128,512]{1,0:T(8,128)S(1)}, u32[]{:S(2)}, u32[]{:S(2)}) collective-permute-start(f32[128,512]{1,0:T(8,128)S(1)} %get-tuple-element.26), channel_id=1, source_target_pairs={{0,16},{8,24},{16,32},{24,40},{32,48},{40,56},{48,0},{56,8},{1,17}... | collective-permute-start | bytes 786440 | tf_op jit(solution)/shard_map/ppermute | solution.py:343
  27.2 14.2 %collective-permute-start.3 = (f32[128,512]{1,0:T(8,128)S(1)}, f32[128,512]{1,0:T(8,128)S(1)}, u32[]{:S(2)}, u32[]{:S(2)}) collective-permute-start(f32[128,512]{1,0:T(8,128)S(1)} %get-tuple-element.27), channel_id=1, source_target_pairs={{0,32},{8,40},{16,48},{24,56},{32,0},{40,8},{48,16},{56,24},{1,33}... | collective-permute-start | bytes 786440 | tf_op jit(solution)/shard_map/ppermute | solution.py:343
  29.9 11.5 %collective-permute-start.4 = (f32[128,512]{1,0:T(8,128)S(1)}, f32[128,512]{1,0:T(8,128)S(1)}, u32[]{:S(2)}, u32[]{:S(2)}) collective-permute-start(f32[128,512]{1,0:T(8,128)S(1)} %get-tuple-element.28), channel_id=1, source_target_pairs={{0,48},{8,56},{16,0},{24,8},{32,16},{40,24},{48,32},{56,40},{1,49}... | collective-permute-start | bytes 786440 | tf_op jit(solution)/shard_map/ppermute | solution.py:343
  31.4 7.0 %collective-permute-start.7 = (f32[328,128]{1,0:T(8,128)S(1)}, f32[328,128]{1,0:T(8,128)S(1)}, u32[]{:S(2)}, u32[]{:S(2)}) collective-permute-start(f32[328,128]{1,0:T(8,128)S(1)} %add.12), channel_id=1, source_target_pairs={{0,2},{1,3},{2,0},{3,1},{4,6},{5,7},{6,4},{7,5},{8,10},{9,11},{10,... | collective-permute-start | bytes 503816 | tf_op jit(solution)/shard_map/ppermute | solution.py:343
  38.4 3.8 %collective-permute-start.8 = (f32[24,128]{1,0:T(8,128)S(1)}, f32[24,128]{1,0:T(8,128)S(1)}, u32[]{:S(2)}, u32[]{:S(2)}) collective-permute-start(f32[24,128]{1,0:T(8,128)S(1)} %slice.4.refs_7_), channel_id=1, source_target_pairs={{0,8},{8,0},{16,24},{24,16},{32,40},{40,32},{48,56},{56,48},{1,9},... | collective-permute-start | bytes 36872 | tf_op jit(solution)/shard_map/ppermute | solution.py:343
  42.9 11.1 %collective-permute-start.10 = (f32[200,256]{1,0:T(8,128)S(1)}, f32[200,256]{1,0:T(8,128)S(1)}, u32[]{:S(2)}, u32[]{:S(2)}) collective-permute-start(f32[200,256]{1,0:T(8,128)S(1)} %get-tuple-element.35), channel_id=1, source_target_pairs={{0,16},{8,24},{16,32},{24,40},{32,48},{40,56},{48,0},{56,8},{1,17}... | collective-permute-start | bytes 614408 | tf_op jit(solution)/shard_map/ppermute | solution.py:343
  43.9 11.8 %collective-permute-start.11 = (f32[200,256]{1,0:T(8,128)S(1)}, f32[200,256]{1,0:T(8,128)S(1)}, u32[]{:S(2)}, u32[]{:S(2)}) collective-permute-start(f32[200,256]{1,0:T(8,128)S(1)} %get-tuple-element.36), channel_id=1, source_target_pairs={{0,32},{8,40},{16,48},{24,56},{32,0},{40,8},{48,16},{56,24},{1,33}... | collective-permute-start | bytes 614408 | tf_op jit(solution)/shard_map/ppermute | solution.py:343
  46.7 9.1 %collective-permute-start.12 = (f32[200,256]{1,0:T(8,128)S(1)}, f32[200,256]{1,0:T(8,128)S(1)}, u32[]{:S(2)}, u32[]{:S(2)}) collective-permute-start(f32[200,256]{1,0:T(8,128)S(1)} %get-tuple-element.37), channel_id=1, source_target_pairs={{0,48},{8,56},{16,0},{24,8},{32,16},{40,24},{48,32},{56,40},{1,49}... | collective-permute-start | bytes 614408 | tf_op jit(solution)/shard_map/ppermute | solution.py:343
  48.1 1.4 %collective-permute-start.13 = (f32[328,128]{1,0:T(8,128)S(1)}, f32[328,128]{1,0:T(8,128)S(1)}, u32[]{:S(2)}, u32[]{:S(2)}) collective-permute-start(f32[328,128]{1,0:T(8,128)S(1)} %add.13.refs_7_), channel_id=1, source_target_pairs={{0,64},{64,0},{1,65},{65,1},{2,66},{66,2},{3,67},{67,3},{4,68},{68... | collective-permute-start | bytes 503816 | tf_op jit(solution)/shard_map/ppermute | solution.py:343
  48.1 5.9 %collective-permute-start.9 = (f32[128,256]{1,0:T(8,128)S(1)}, f32[128,256]{1,0:T(8,128)S(1)}, u32[]{:S(2)}, u32[]{:S(2)}) collective-permute-start(f32[128,256]{1,0:T(8,128)S(1)} %get-tuple-element.33), channel_id=1, source_target_pairs={{0,8},{8,0},{16,24},{24,16},{32,40},{40,32},{48,56},{56,48},{1,9},... | collective-permute-start | bytes 393224 | tf_op jit(solution)/shard_map/ppermute | solution.py:343

commit v4 on v3

--- a/solution.py
+++ b/solution.py
@@ -12,8 +12,8 @@
 BF16 = jnp.bfloat16
 MIB = 1024 * 1024
 BIG = 50 * MIB
-OWN = 42 * MIB
-WORD = 50 * MIB
+OWN = 50 * MIB
+WORD = 54 * MIB
 FRONT_TILE = 1024
 TOP = 128
 NT = (((1,), (1,)), ((), ()))
@@ -81,12 +81,17 @@
     return steps
 
 
-def front_kernel(pos_ref, word_ref, off_ref, data_ref, ctx_ref, mat_ref, *refs):
-    ctx_out, a_out, out_ref, d_buf, c_buf, m_buf, d_sem, c_sem, m_sem = refs
+def position():
+    row = lax.axis_index("rows")
+    return lax.axis_index("section"), lax.div(row, 2), lax.rem(row, 2)
+
+
+def front_kernel(pos, word_ref, off_ref, data_ref, ctx_ref, mat_ref, *refs):
+    ctx_out, out_ref, d_buf, c_buf, m_buf, d_sem, c_sem, m_sem = refs
     steps, _, tile = d_buf.shape
     words, offsets = word_ref.shape[1], off_ref.shape[0]
     rank = word_ref.shape[0]
-    section = pos_ref[0]
+    section = pos[0]
     half = steps // 2
     plan = []
     for i in range(steps):
@@ -104,7 +109,6 @@
     wide_w = dot(w, spread_w)
     wide_o = dot_tn(o, spread_o)
     a = (wide_w * wide_o).astype(BF16)
-    a_out[...] = a
     gram_w = dot_nt(w, w)
     gram_o = dot_tn(o, o)
     m_hi, m_rest = split_diagonal(gram_w * gram_o)
@@ -150,7 +154,7 @@
         out_ref[at, pl.ds(0, part)] = off[:, k * 128 : k * 128 + part]
 
 
-def front_part(pos, data, matrix, word, off_t, ctx):
+def front_part(data, matrix, word, off_t, ctx):
     rank, words = word.shape
     offsets = off_t.shape[0]
     rows, width = data.shape
@@ -161,14 +165,13 @@
     vmem = pl.BlockSpec(memory_space=pltpu.VMEM)
     anywhere = pl.BlockSpec(memory_space=pl.ANY)
     return pl.pallas_call(
-        front_kernel,
+        lambda *refs: front_kernel(position(), *refs),
         out_shape=[
             jax.ShapeDtypeStruct((rank, width // 2), F32),
-            jax.ShapeDtypeStruct((rank, rows), BF16),
             jax.ShapeDtypeStruct((out_rows, words), F32),
         ],
-        in_specs=[pl.BlockSpec(memory_space=pltpu.SMEM), vmem, vmem] + [anywhere] * 3,
-        out_specs=[vmem] * 3,
+        in_specs=[vmem, vmem] + [anywhere] * 3,
+        out_specs=[vmem] * 2,
         scratch_shapes=[
             pltpu.VMEM((steps, rows, tile), BF16),
             pltpu.VMEM((steps, rank, tile), BF16),
@@ -182,14 +185,14 @@
             flops=3 * rank * width * (rows + rank), bytes_accessed=rows * width * 2 + rank * width * 2, transcendentals=0
         ),
         name="front",
-    )(pos, word, off_t, data, ctx, matrix)
-
-
-def own_kernel(pos_ref, word_ref, off_ref, a_ref, data_ref, ctx_ref, mat_ref, after_ref, out_ref, *refs):
+    )(word, off_t, data, ctx, matrix)
+
+
+def own_kernel(pos, word_ref, off_ref, data_ref, ctx_ref, mat_ref, after_ref, out_ref, *refs):
     del after_ref
     d_buf, c_buf, m_buf, d_sem, c_sem, m_sem = refs
     steps, _, tile = d_buf.shape
-    base = pos_ref[0] * (steps * tile)
+    base = pos[0] * (steps * tile)
     plan = []
     for i in range(steps):
         here = pl.ds(i * tile, tile)
@@ -202,7 +205,8 @@
     loads = start_loads(plan)
     w = word_ref[...]
     o = off_ref[...]
-    a = a_ref[...]
+    words, offsets = w.shape[1], o.shape[0]
+    a = (dot(w, word_spread(words, offsets)) * dot_tn(o, offset_spread(words, offsets))).astype(BF16)
     hi, rest = split_diagonal(dot_nt(w, w) * (dot_tn(o, o) + 1.0))
     for i in range(steps):
         for c in loads[i]:
@@ -212,7 +216,7 @@
         out_ref[:, pl.ds(i * tile, tile)] = total
 
 
-def own_part(pos, data, matrix, word, off_t, ctx, a, after):
+def own_part(data, matrix, word, off_t, ctx, after):
     rank, words = word.shape
     rows, width = data.shape
     half = width // 2
@@ -222,9 +226,9 @@
     anywhere = pl.BlockSpec(memory_space=pl.ANY)
     flops = 100 * rank * half * (rows + 2 * rank)
     return pl.pallas_call(
-        own_kernel,
+        lambda *refs: own_kernel(position(), *refs),
         out_shape=jax.ShapeDtypeStruct((rank, half), F32),
-        in_specs=[pl.BlockSpec(memory_space=pltpu.SMEM), vmem, vmem, vmem] + [anywhere] * 4,
+        in_specs=[vmem, vmem] + [anywhere] * 4,
         out_specs=vmem,
         scratch_shapes=[
             pltpu.VMEM((steps, rows, tile), BF16),
@@ -235,34 +239,34 @@
         compiler_params=pltpu.CompilerParams(vmem_limit_bytes=OWN),
         cost_estimate=pl.CostEstimate(flops=flops, bytes_accessed=rows * half * 100 + rank * half * 300, transcendentals=0),
         name="own_half",
-    )(pos, word, off_t, a, data, ctx, matrix, after)
-
-
-def whole_call(kernel, outs, name, pos, *args, after=()):
+    )(word, off_t, data, ctx, matrix, after)
+
+
+def whole_call(kernel, outs, name, *args, after=()):
     vmem = pl.BlockSpec(memory_space=pltpu.VMEM)
     anywhere = pl.BlockSpec(memory_space=pl.ANY)
-    n = 1 + len(args)
+    n = len(args)
 
     def body(*refs):
-        kernel(*refs[:n], *refs[n + len(after) :])
+        kernel(position(), *refs[:n], *refs[n + len(after) :])
 
     return pl.pallas_call(
         body,
         out_shape=[jax.ShapeDtypeStruct(o, F32) for o in outs],
-        in_specs=[pl.BlockSpec(memory_space=pltpu.SMEM)] + [vmem] * len(args) + [anywhere] * len(after),
+        in_specs=[vmem] * len(args) + [anywhere] * len(after),
         out_specs=[vmem] * len(outs),
         compiler_params=pltpu.CompilerParams(vmem_limit_bytes=24 * MIB),
         cost_estimate=pl.CostEstimate(flops=1024, bytes_accessed=1024, transcendentals=0),
         name=name,
-    )(pos, *args, *after)
+    )(*args, *after)
 
 
 def lanes(start, width):
     return pl.ds(pl.multiple_of(start, 128), width)
 
 
-def first_sum(pos_ref, own_ref, got_ref, part_ref, more_ref, x1_ref, x2_ref, x3_ref, y_ref, kx_ref, ky_ref, sum_ref):
-    x, y = pos_ref[1], pos_ref[2]
+def first_sum(pos, own_ref, got_ref, part_ref, more_ref, x1_ref, x2_ref, x3_ref, y_ref, kx_ref, ky_ref, sum_ref):
+    x, y = pos[1], pos[2]
     top, width = kx_ref.shape
     low, span = ky_ref.shape
     block = span // 4
@@ -276,9 +280,9 @@
     sum_ref[...] = part_ref[...] + more_ref[...]
 
 
-def middle_sum(pos_ref, k_ref, a_ref, b_ref, c_ref, l_ref, g_ref, off_ref, more_ref, *refs):
+def middle_sum(pos, k_ref, a_ref, b_ref, c_ref, l_ref, g_ref, off_ref, more_ref, *refs):
     sx_ref, kx_ref, x1_ref, x2_ref, x3_ref, ky_ref = refs
-    x, y = pos_ref[1], pos_ref[2]
+    x, y = pos[1], pos[2]
     block = sx_ref.shape[1]
     low = l_ref.shape[0]
     for hop, ref in ((1, x1_ref), (3, x3_ref), (2, x2_ref), (0, ky_ref)):
@@ -297,7 +301,7 @@
         ref[...] = (k_ref[:, at] + a_ref[:, at]) + (b_ref[:, at] + c_ref[:, at])
 
 
-def last_sum(scales, pos_ref, k_ref, a_ref, l_ref, b_ref, c_ref, d_ref, w_ref, v_ref, ctx_ref, word_ref, off_ref):
+def last_sum(scales, pos, k_ref, a_ref, l_ref, b_ref, c_ref, d_ref, w_ref, v_ref, ctx_ref, word_ref, off_ref):
     top = k_ref.shape[0]
     rank = ctx_ref.shape[0]
     low = rank - top
@@ -349,15 +353,12 @@
     all_words = words * lax.axis_size("rows")
     all_offsets = offsets * lax.axis_size("section")
     all_contexts = width * lax.axis_size("cols")
-    section = lax.axis_index("section")
-    row = lax.axis_index("rows")
-    pos = jnp.stack([section, row // 2, row % 2]).astype(jnp.int32)
     data = tensor_data.reshape(words * offsets, width)
     off_t = offset_factor.T
-    other, a, part = front_part(pos, data, matrix_data, word_factor, off_t, context_factor)
+    other, part = front_part(data, matrix_data, word_factor, off_t, context_factor)
     got = send(other, "section", SWAP)
     more = send(part, "cols", Y_HIGH)
-    own = own_part(pos, data, matrix_data, word_factor, off_t, context_factor, a, part)
+    own = own_part(data, matrix_data, word_factor, off_t, context_factor, part)
 
     top = TOP
     low = rank - top
@@ -365,7 +366,7 @@
     extra = chunk_count(rank) * offsets
     x1, x2, x3, y1, kx, ky, part = whole_call(
         first_sum, [(top, 2 * block)] * 3 + [(low, 4 * block), (top, 2 * block), (low, 4 * block), part.shape],
-        "first_sum", pos, own, got, part, more,
+        "first_sum", own, got, part, more,
     )
     f1 = send(x1, "rows", X_HOP[1])
     f3 = send(x3, "rows", X_HOP[3])
@@ -378,7 +379,7 @@
     other_word = send(word, "section", SWAP)
     longer = (-(-low // 8) * 8 + extra, block)
     sx, kx, x1, x2, x3, ky = whole_call(
-        middle_sum, [(top, block)] * 2 + [longer] * 4, "middle_sum", pos, kx, f1, f2, f3, ky, g, off, more
+        middle_sum, [(top, block)] * 2 + [longer] * 4, "middle_sum", kx, f1, f2, f3, ky, g, off, more
     )
     f1 = send(x1, "rows", X_HOP[1])
     f3 = send(x3, "rows", X_HOP[3])
@@ -392,7 +393,7 @@
     grad_context, grad_word, grad_offset = whole_call(
         functools.partial(last_sum, scales),
         [(rank, block), (rank, words), (offsets, rank)],
-        "last_sum", pos, kx, g, ky, f1, f2, f3, word, other_word,
+        "last_sum", kx, g, ky, f1, f2, f3, word, other_word,
     )
     return (grad_word, grad_context, grad_offset.T)
 

time: 57.4 us -> 54.2 us (0.944)
  local copies, waits for them, and re-layouts: 2.64 us -> 0.94 us
  Pallas kernels: 18.1 us -> 16.8 us
    unnamed x14 -> x8, local copies, waits for them, and re-layouts: 2.63 us -> 0.93 us
    pallas_call x3, Pallas kernels: 2.98 us -> 1.38 us  [whole_call(): pl.pallas_call(body, out_shape=[jax.ShapeDtypeStruct(o, F32) for o in out...]
  transfers between devices with their start and end apart: 14 -> 14, of which waited for: 6 -> 6; matrix products, arithmetic and copies ran while one was open for 0% -> 0% of each run, Pallas kernels for 9% -> 8%
where the time goes in v4:
time: 54.2 us; the launch traced here: 54 us
  starting transfers between devices  23.3 us (43%)
  Pallas kernels  16.8 us (31%)
  waiting for transfers between devices  12.2 us (23%)
  local copies, waits for them, and re-layouts  0.94 us (2%)
  between operations  0.74 us (1%)
    ppermute x14, starting transfers between devices, send(): return lax.ppermute(v, axis, perm)  23.3 us
    ppermute x14, waiting for transfers between devices, send(): return lax.ppermute(v, axis, perm)  12.2 us
    pallas_call x1, Pallas kernels, front_part(): pl.pallas_call(lambda *refs: front_kernel(position(), *refs), out_shape=[...  11 us
    pallas_call x1, Pallas kernels, own_part(): pl.pallas_call(lambda *refs: own_kernel(position(), *refs), out_shape=jax...  4.43 us
    pallas_call x3, Pallas kernels, whole_call(): pl.pallas_call(body, out_shape=[jax.ShapeDtypeStruct(o, F32) for o in out...  1.38 us
  transfers between devices with their start and end apart: 14, of which 6 were waited for; matrix products, arithmetic and copies ran while one was open for 0% of the time, Pallas kernels for 8%

profile of v4, /device:TPU:0, one launch (start us, length us, event | category | flops | bytes accessed | tf_op | source)
XLA Modules:
  0.0 54.0 jit_solution(1911884311095324229)
XLA Ops:
  0.7 11.0 %front.1 = (f32[300,2048]{1,0:T(8,128)}, f32[328,128]{1,0:T(8,128)}) custom-call(bf16[300,128]{1,0:T(8,128)(2,1)} %refs_0_.3, bf16[8,300]{1,0:T(8,128)(2,1)} %bitcast.3, bf16[1024,4096]{1,0:T(8,128)(2,1)} %bitcast.5, bf16[300,4096]{1,0:T(8,128)(2,1)} %refs_3_.3, bf16[128,2048]{1,0:T(8,128)(2,1)} %refs_4_.3), custom_call_target="tpu_custom_call" | custom-call | flops 4880793600 | bytes 10846208 | tf_op jit(solution)/shard_map/front/pallas_call | solution.py:167
  11.7 3.4 %collective-permute-start.1 = (f32[328,128]{1,0:T(8,128)}, f32[328,128]{1,0:T(8,128)S(1)}, u32[]{:S(2)}, u32[]{:S(2)}) collective-permute-start(f32[328,128]{1,0:T(8,128)} %get-tuple-element.21.refs_5_.refs_2_), channel_id=1, source_target_pairs={{0,4},{1,5},{2,6},{3,7},{4,0},{5,1},{6,2},{7,3},{8,12},{9,13},{10,... | collective-permute-start | bytes 503816 | tf_op jit(solution)/shard_map/ppermute | solution.py:347
  15.1 0.9 %copy-done = f32[328,128]{1,0:T(8,128)S(1)} copy-done((f32[328,128]{1,0:T(8,128)S(1)}, f32[328,128]{1,0:T(8,128)}, u32[]{:S(2)}) %copy-start) | copy-done | bytes 167960
  16.0 4.4 %own_half.1.refs_0_ = f32[300,2048]{1,0:T(8,128)S(1)} custom-call(bf16[300,128]{1,0:T(8,128)(2,1)S(1)} %copy-done.2, bf16[8,300]{1,0:T(8,128)(2,1)S(1)} %bitcast.4, bf16[1024,4096]{1,0:T(8,128)(2,1)} %bitcast.6, bf16[300,4096]{1,0:T(8,128)(2,1)} %refs_3_.3, bf16[128,2048]{1,0:T(8,128)(2,1)S(1)} %copy-done.1, f32[328,128]{1,0:T(8,128)S(1)} %copy-done), custom_call_target="tpu_custom_call" | custom-call | flops 99778560000 | bytes 394035200 | tf_op jit(solution)/shard_map/own_half/pallas_call | solution.py:228
  20.5 0.3 first_sum.1
  20.8 0.8 %collective-permute-start.5 = (f32[172,1024]{1,0:T(8,128)S(1)}, f32[172,1024]{1,0:T(8,128)S(1)}, u32[]{:S(2)}, u32[]{:S(2)}) collective-permute-start(f32[172,1024]{1,0:T(8,128)S(1)} %get-tuple-element.28), channel_id=1, source_target_pairs={{0,8},{8,0},{16,24},{24,16},{32,40},{40,32},{48,56},{56,48},{1,9},... | collective-permute-start | bytes 2113544 | tf_op jit(solution)/shard_map/ppermute | solution.py:347
  21.6 1.9 %collective-permute-start.6 = (f32[328,128]{1,0:T(8,128)S(1)}, f32[328,128]{1,0:T(8,128)S(1)}, u32[]{:S(2)}, u32[]{:S(2)}) collective-permute-start(f32[328,128]{1,0:T(8,128)S(1)} %get-tuple-element.29), channel_id=1, source_target_pairs={{0,1},{1,0},{2,3},{3,2},{4,5},{5,4},{6,7},{7,6},{8,9},{9,8},{10,11... | collective-permute-start | bytes 503816 | tf_op jit(solution)/shard_map/ppermute | solution.py:347
  23.5 1.5 %collective-permute-start.2 = (f32[128,512]{1,0:T(8,128)S(1)}, f32[128,512]{1,0:T(8,128)S(1)}, u32[]{:S(2)}, u32[]{:S(2)}) collective-permute-start(f32[128,512]{1,0:T(8,128)S(1)} %get-tuple-element.24), channel_id=1, source_target_pairs={{0,16},{8,24},{16,32},{24,40},{32,48},{40,56},{48,0},{56,8},{1,17}... | collective-permute-start | bytes 786440 | tf_op jit(solution)/shard_map/ppermute | solution.py:347
  25.0 2.7 %collective-permute-start.3 = (f32[128,512]{1,0:T(8,128)S(1)}, f32[128,512]{1,0:T(8,128)S(1)}, u32[]{:S(2)}, u32[]{:S(2)}) collective-permute-start(f32[128,512]{1,0:T(8,128)S(1)} %get-tuple-element.25), channel_id=1, source_target_pairs={{0,32},{8,40},{16,48},{24,56},{32,0},{40,8},{48,16},{56,24},{1,33}... | collective-permute-start | bytes 786440 | tf_op jit(solution)/shard_map/ppermute | solution.py:347
  27.7 1.4 %collective-permute-start.4 = (f32[128,512]{1,0:T(8,128)S(1)}, f32[128,512]{1,0:T(8,128)S(1)}, u32[]{:S(2)}, u32[]{:S(2)}) collective-permute-start(f32[128,512]{1,0:T(8,128)S(1)} %get-tuple-element.26), channel_id=1, source_target_pairs={{0,48},{8,56},{16,0},{24,8},{32,16},{40,24},{48,32},{56,40},{1,49}... | collective-permute-start | bytes 786440 | tf_op jit(solution)/shard_map/ppermute | solution.py:347
  29.2 3.7 %collective-permute-start.7 = (f32[328,128]{1,0:T(8,128)S(1)}, f32[328,128]{1,0:T(8,128)S(1)}, u32[]{:S(2)}, u32[]{:S(2)}) collective-permute-start(f32[328,128]{1,0:T(8,128)S(1)} %add.6), channel_id=1, source_target_pairs={{0,2},{1,3},{2,0},{3,1},{4,6},{5,7},{6,4},{7,5},{8,10},{9,11},{10,... | collective-permute-start | bytes 503816 | tf_op jit(solution)/shard_map/ppermute | solution.py:347
  32.8 3.5 %collective-permute-done.7 = f32[328,128]{1,0:T(8,128)S(1)} collective-permute-done((f32[328,128]{1,0:T(8,128)S(1)}, f32[328,128]{1,0:T(8,128)S(1)}, u32[]{:S(2)}, u32[]{:S(2)}) %collective-permute-start.7) | collective-permute-done | bytes 167968 | tf_op jit(solution)/shard_map/ppermute | solution.py:347
  36.4 1.4 %collective-permute-start.8 = (f32[24,128]{1,0:T(8,128)S(1)}, f32[24,128]{1,0:T(8,128)S(1)}, u32[]{:S(2)}, u32[]{:S(2)}) collective-permute-start(f32[24,128]{1,0:T(8,128)S(1)} %slice.4.refs_6_), channel_id=1, source_target_pairs={{0,8},{8,0},{16,24},{24,16},{32,40},{40,32},{48,56},{56,48},{1,9},... | collective-permute-start | bytes 36872 | tf_op jit(solution)/shard_map/ppermute | solution.py:347
  37.8 1.6 %collective-permute-done.3.refs_2_ = f32[128,512]{1,0:T(8,128)S(1)} collective-permute-done((f32[128,512]{1,0:T(8,128)S(1)}, f32[128,512]{1,0:T(8,128)S(1)}, u32[]{:S(2)}, u32[]{:S(2)}) %collective-permute-start.3) | collective-permute-done | bytes 262176 | tf_op jit(solution)/shard_map/ppermute | solution.py:347
  39.4 0.7 %collective-permute-done.8.refs_7_ = f32[24,128]{1,0:T(8,128)S(1)} collective-permute-done((f32[24,128]{1,0:T(8,128)S(1)}, f32[24,128]{1,0:T(8,128)S(1)}, u32[]{:S(2)}, u32[]{:S(2)}) %collective-permute-start.8) | collective-permute-done | bytes 12320 | tf_op jit(solution)/shard_map/ppermute | solution.py:347
  40.2 0.2 middle_sum.1
  40.4 1.1 %collective-permute-start.10 = (f32[200,256]{1,0:T(8,128)S(1)}, f32[200,256]{1,0:T(8,128)S(1)}, u32[]{:S(2)}, u32[]{:S(2)}) collective-permute-start(f32[200,256]{1,0:T(8,128)S(1)} %get-tuple-element.33), channel_id=1, source_target_pairs={{0,16},{8,24},{16,32},{24,40},{32,48},{40,56},{48,0},{56,8},{1,17}... | collective-permute-start | bytes 614408 | tf_op jit(solution)/shard_map/ppermute | solution.py:347
  41.4 2.7 %collective-permute-start.11 = (f32[200,256]{1,0:T(8,128)S(1)}, f32[200,256]{1,0:T(8,128)S(1)}, u32[]{:S(2)}, u32[]{:S(2)}) collective-permute-start(f32[200,256]{1,0:T(8,128)S(1)} %get-tuple-element.34), channel_id=1, source_target_pairs={{0,32},{8,40},{16,48},{24,56},{32,0},{40,8},{48,16},{56,24},{1,33}... | collective-permute-start | bytes 614408 | tf_op jit(solution)/shard_map/ppermute | solution.py:347
  44.1 1.4 %collective-permute-start.12 = (f32[200,256]{1,0:T(8,128)S(1)}, f32[200,256]{1,0:T(8,128)S(1)}, u32[]{:S(2)}, u32[]{:S(2)}) collective-permute-start(f32[200,256]{1,0:T(8,128)S(1)} %get-tuple-element.35), channel_id=1, source_target_pairs={{0,48},{8,56},{16,0},{24,8},{32,16},{40,24},{48,32},{56,40},{1,49}... | collective-permute-start | bytes 614408 | tf_op jit(solution)/shard_map/ppermute | solution.py:347
  45.6 1.3 %collective-permute-start.9 = (f32[128,256]{1,0:T(8,128)S(1)}, f32[128,256]{1,0:T(8,128)S(1)}, u32[]{:S(2)}, u32[]{:S(2)}) collective-permute-start(f32[128,256]{1,0:T(8,128)S(1)} %get-tuple-element.31), channel_id=1, source_target_pairs={{0,8},{8,0},{16,24},{24,16},{32,40},{40,32},{48,56},{56,48},{1,9},... | collective-permute-start | bytes 393224 | tf_op jit(solution)/shard_map/ppermute | solution.py:347
  46.9 0.1 collective-permute-done.13.refs_7_
  47.0 4.5 %collective-permute-done.9.refs_1_ = f32[128,256]{1,0:T(8,128)S(1)} collective-permute-done((f32[128,256]{1,0:T(8,128)S(1)}, f32[128,256]{1,0:T(8,128)S(1)}, u32[]{:S(2)}, u32[]{:S(2)}) %collective-permute-start.9) | collective-permute-done | bytes 131104 | tf_op jit(solution)/shard_map/ppermute | solution.py:347
  51.5 1.7 %collective-permute-done.11.refs_4_ = f32[200,256]{1,0:T(8,128)S(1)} collective-permute-done((f32[200,256]{1,0:T(8,128)S(1)}, f32[200,256]{1,0:T(8,128)S(1)}, u32[]{:S(2)}, u32[]{:S(2)}) %collective-permute-start.11) | collective-permute-done | bytes 204832 | tf_op jit(solution)/shard_map/ppermute | solution.py:347
  53.2 0.9 %last_sum.1 = (f32[300,256]{1,0:T(8,128)}, f32[300,128]{1,0:T(8,128)}, f32[8,300]{1,0:T(8,128)}) custom-call(f32[128,256]{1,0:T(8,128)S(1)} %get-tuple-element.30.refs_0_, f32[128,256]{1,0:T(8,128)S(1)} %collective-permute-done.9.refs_1_, f32[200,256]{1,0:T(8,128)S(1)} %get-tuple-element.32.refs_2_, f32[200,256]{1,0:T(8,128)S(1)} %collective-permute-done.10.refs_3_, ...), custom_call_target="tpu_custom_call" | custom-call | flops 1024 | bytes 1024 | tf_op jit(solution)/shard_map/last_sum/pallas_call | solution.py:253
  (20 shorter events, 0.1 us)
Async XLA Ops:
  0.6 14.4 %copy-start.1 = (bf16[128,2048]{1,0:T(8,128)(2,1)S(1)}, bf16[128,2048]{1,0:T(8,128)(2,1)}, u32[]{:S(2)}) copy-start(bf16[128,2048]{1,0:T(8,128)(2,1)} %refs_4_.3) | copy-start | bytes 1572868
  0.6 14.4 %copy-start.2 = (bf16[300,128]{1,0:T(8,128)(2,1)S(1)}, bf16[300,128]{1,0:T(8,128)(2,1)}, u32[]{:S(2)}) copy-start(bf16[300,128]{1,0:T(8,128)(2,1)} %refs_0_.3) | copy-start | bytes 230404
  0.7 14.4 %copy-start.3 = (bf16[300,8]{0,1:T(8,128)(2,1)S(1)}, bf16[300,8]{0,1:T(8,128)(2,1)}, u32[]{:S(2)}) copy-start(bf16[300,8]{0,1:T(8,128)(2,1)} %param.9) | copy-start | bytes 14404
  11.7 8.7 %collective-permute-start.1 = (f32[328,128]{1,0:T(8,128)}, f32[328,128]{1,0:T(8,128)S(1)}, u32[]{:S(2)}, u32[]{:S(2)}) collective-permute-start(f32[328,128]{1,0:T(8,128)} %get-tuple-element.21.refs_5_.refs_2_), channel_id=1, source_target_pairs={{0,4},{1,5},{2,6},{3,7},{4,0},{5,1},{6,2},{7,3},{8,12},{9,13},{10,... | collective-permute-start | bytes 503816 | tf_op jit(solution)/shard_map/ppermute | solution.py:347
  15.0 5.4 %collective-permute-start = (f32[300,2048]{1,0:T(8,128)}, f32[300,2048]{1,0:T(8,128)S(1)}, u32[]{:S(2)}, u32[]{:S(2)}) collective-permute-start(f32[300,2048]{1,0:T(8,128)} %get-tuple-element.22), channel_id=1, source_target_pairs={{0,64},{64,0},{1,65},{65,1},{2,66},{66,2},{3,67},{67,3},{4,68},{68... | collective-permute-start | bytes 7372808 | tf_op jit(solution)/shard_map/ppermute | solution.py:347
  15.1 0.9 %copy-start = (f32[328,128]{1,0:T(8,128)S(1)}, f32[328,128]{1,0:T(8,128)}, u32[]{:S(2)}) copy-start(f32[328,128]{1,0:T(8,128)} %get-tuple-element.21.refs_5_.refs_2_) | copy-start | bytes 503812
  20.8 19.4 %collective-permute-start.5 = (f32[172,1024]{1,0:T(8,128)S(1)}, f32[172,1024]{1,0:T(8,128)S(1)}, u32[]{:S(2)}, u32[]{:S(2)}) collective-permute-start(f32[172,1024]{1,0:T(8,128)S(1)} %get-tuple-element.28), channel_id=1, source_target_pairs={{0,8},{8,0},{16,24},{24,16},{32,40},{40,32},{48,56},{56,48},{1,9},... | collective-permute-start | bytes 2113544 | tf_op jit(solution)/shard_map/ppermute | solution.py:347
  21.6 7.6 %collective-permute-start.6 = (f32[328,128]{1,0:T(8,128)S(1)}, f32[328,128]{1,0:T(8,128)S(1)}, u32[]{:S(2)}, u32[]{:S(2)}) collective-permute-start(f32[328,128]{1,0:T(8,128)S(1)} %get-tuple-element.29), channel_id=1, source_target_pairs={{0,1},{1,0},{2,3},{3,2},{4,5},{5,4},{6,7},{7,6},{8,9},{9,8},{10,11... | collective-permute-start | bytes 503816 | tf_op jit(solution)/shard_map/ppermute | solution.py:347
  23.5 14.3 %collective-permute-start.2 = (f32[128,512]{1,0:T(8,128)S(1)}, f32[128,512]{1,0:T(8,128)S(1)}, u32[]{:S(2)}, u32[]{:S(2)}) collective-permute-start(f32[128,512]{1,0:T(8,128)S(1)} %get-tuple-element.24), channel_id=1, source_target_pairs={{0,16},{8,24},{16,32},{24,40},{32,48},{40,56},{48,0},{56,8},{1,17}... | collective-permute-start | bytes 786440 | tf_op jit(solution)/shard_map/ppermute | solution.py:347
  25.0 14.4 %collective-permute-start.3 = (f32[128,512]{1,0:T(8,128)S(1)}, f32[128,512]{1,0:T(8,128)S(1)}, u32[]{:S(2)}, u32[]{:S(2)}) collective-permute-start(f32[128,512]{1,0:T(8,128)S(1)} %get-tuple-element.25), channel_id=1, source_target_pairs={{0,32},{8,40},{16,48},{24,56},{32,0},{40,8},{48,16},{56,24},{1,33}... | collective-permute-start | bytes 786440 | tf_op jit(solution)/shard_map/ppermute | solution.py:347
  27.7 11.7 %collective-permute-start.4 = (f32[128,512]{1,0:T(8,128)S(1)}, f32[128,512]{1,0:T(8,128)S(1)}, u32[]{:S(2)}, u32[]{:S(2)}) collective-permute-start(f32[128,512]{1,0:T(8,128)S(1)} %get-tuple-element.26), channel_id=1, source_target_pairs={{0,48},{8,56},{16,0},{24,8},{32,16},{40,24},{48,32},{56,40},{1,49}... | collective-permute-start | bytes 786440 | tf_op jit(solution)/shard_map/ppermute | solution.py:347
  29.2 7.2 %collective-permute-start.7 = (f32[328,128]{1,0:T(8,128)S(1)}, f32[328,128]{1,0:T(8,128)S(1)}, u32[]{:S(2)}, u32[]{:S(2)}) collective-permute-start(f32[328,128]{1,0:T(8,128)S(1)} %add.6), channel_id=1, source_target_pairs={{0,2},{1,3},{2,0},{3,1},{4,6},{5,7},{6,4},{7,5},{8,10},{9,11},{10,... | collective-permute-start | bytes 503816 | tf_op jit(solution)/shard_map/ppermute | solution.py:347
  36.4 3.8 %collective-permute-start.8 = (f32[24,128]{1,0:T(8,128)S(1)}, f32[24,128]{1,0:T(8,128)S(1)}, u32[]{:S(2)}, u32[]{:S(2)}) collective-permute-start(f32[24,128]{1,0:T(8,128)S(1)} %slice.4.refs_6_), channel_id=1, source_target_pairs={{0,8},{8,0},{16,24},{24,16},{32,40},{40,32},{48,56},{56,48},{1,9},... | collective-permute-start | bytes 36872 | tf_op jit(solution)/shard_map/ppermute | solution.py:347
  40.4 11.1 %collective-permute-start.10 = (f32[200,256]{1,0:T(8,128)S(1)}, f32[200,256]{1,0:T(8,128)S(1)}, u32[]{:S(2)}, u32[]{:S(2)}) collective-permute-start(f32[200,256]{1,0:T(8,128)S(1)} %get-tuple-element.33), channel_id=1, source_target_pairs={{0,16},{8,24},{16,32},{24,40},{32,48},{40,56},{48,0},{56,8},{1,17}... | collective-permute-start | bytes 614408 | tf_op jit(solution)/shard_map/ppermute | solution.py:347
  41.4 11.7 %collective-permute-start.11 = (f32[200,256]{1,0:T(8,128)S(1)}, f32[200,256]{1,0:T(8,128)S(1)}, u32[]{:S(2)}, u32[]{:S(2)}) collective-permute-start(f32[200,256]{1,0:T(8,128)S(1)} %get-tuple-element.34), channel_id=1, source_target_pairs={{0,32},{8,40},{16,48},{24,56},{32,0},{40,8},{48,16},{56,24},{1,33}... | collective-permute-start | bytes 614408 | tf_op jit(solution)/shard_map/ppermute | solution.py:347
  44.1 9.0 %collective-permute-start.12 = (f32[200,256]{1,0:T(8,128)S(1)}, f32[200,256]{1,0:T(8,128)S(1)}, u32[]{:S(2)}, u32[]{:S(2)}) collective-permute-start(f32[200,256]{1,0:T(8,128)S(1)} %get-tuple-element.35), channel_id=1, source_target_pairs={{0,48},{8,56},{16,0},{24,8},{32,16},{40,24},{48,32},{56,40},{1,49}... | collective-permute-start | bytes 614408 | tf_op jit(solution)/shard_map/ppermute | solution.py:347
  45.6 1.4 %collective-permute-start.13 = (f32[328,128]{1,0:T(8,128)S(1)}, f32[328,128]{1,0:T(8,128)S(1)}, u32[]{:S(2)}, u32[]{:S(2)}) collective-permute-start(f32[328,128]{1,0:T(8,128)S(1)} %add.7.refs_6_), channel_id=1, source_target_pairs={{0,64},{64,0},{1,65},{65,1},{2,66},{66,2},{3,67},{67,3},{4,68},{68... | collective-permute-start | bytes 503816 | tf_op jit(solution)/shard_map/ppermute | solution.py:347
  45.6 5.9 %collective-permute-start.9 = (f32[128,256]{1,0:T(8,128)S(1)}, f32[128,256]{1,0:T(8,128)S(1)}, u32[]{:S(2)}, u32[]{:S(2)}) collective-permute-start(f32[128,256]{1,0:T(8,128)S(1)} %get-tuple-element.31), channel_id=1, source_target_pairs={{0,8},{8,0},{16,24},{24,16},{32,40},{40,32},{48,56},{56,48},{1,9},... | collective-permute-start | bytes 393224 | tf_op jit(solution)/shard_map/ppermute | solution.py:347

commit v5 on v4

--- a/solution.py
+++ b/solution.py
@@ -224,7 +224,7 @@
     steps = half // tile
     vmem = pl.BlockSpec(memory_space=pltpu.VMEM)
     anywhere = pl.BlockSpec(memory_space=pl.ANY)
-    flops = 100 * rank * half * (rows + 2 * rank)
+    flops = 20 * rank * half * (rows + 2 * rank)
     return pl.pallas_call(
         lambda *refs: own_kernel(position(), *refs),
         out_shape=jax.ShapeDtypeStruct((rank, half), F32),
@@ -237,7 +237,7 @@
         ]
         + [pltpu.SemaphoreType.DMA((steps,))] * 3,
         compiler_params=pltpu.CompilerParams(vmem_limit_bytes=OWN),
-        cost_estimate=pl.CostEstimate(flops=flops, bytes_accessed=rows * half * 100 + rank * half * 300, transcendentals=0),
+        cost_estimate=pl.CostEstimate(flops=flops, bytes_accessed=rows * half * 20 + rank * half * 60, transcendentals=0),
         name="own_half",
     )(word, off_t, data, ctx, matrix, after)
 
@@ -358,7 +358,7 @@
     other, part = front_part(data, matrix_data, word_factor, off_t, context_factor)
     got = send(other, "section", SWAP)
     more = send(part, "cols", Y_HIGH)
-    own = own_part(data, matrix_data, word_factor, off_t, context_factor, part)
+    own = own_part(data, matrix_data, word_factor, off_t, context_factor, other)
 
     top = TOP
     low = rank - top

time: 54.2 us -> 53.3 us (0.983)
  waiting for transfers between devices: 12.2 us -> 13.4 us
  starting transfers between devices: 23.3 us -> 22.1 us
  local copies, waits for them, and re-layouts: 0.94 us -> 0.02 us
    ppermute x14, waiting for transfers between devices: 12.2 us -> 13.4 us  [send(): return lax.ppermute(v, axis, perm)]
    ppermute x14, starting transfers between devices: 23.3 us -> 22.1 us  [send(): return lax.ppermute(v, axis, perm)]
    unnamed x8, local copies, waits for them, and re-layouts: 0.93 us -> 0.02 us
  transfers between devices with their start and end apart: 14 -> 14, of which waited for: 6 -> 7; matrix products, arithmetic and copies ran while one was open for 0% -> 0% of each run, Pallas kernels for 8% -> 8%
where the time goes in v5:
time: 53.3 us; the launch traced here: 53.2 us
  starting transfers between devices  22.1 us (41%)
  Pallas kernels  16.8 us (32%)
  waiting for transfers between devices  13.4 us (25%)
  between operations  0.72 us (1%)
    ppermute x14, starting transfers between devices, send(): return lax.ppermute(v, axis, perm)  22.1 us
    ppermute x14, waiting for transfers between devices, send(): return lax.ppermute(v, axis, perm)  13.4 us
    pallas_call x1, Pallas kernels, front_part(): pl.pallas_call(lambda *refs: front_kernel(position(), *refs), out_shape=[...  11 us
    pallas_call x1, Pallas kernels, own_part(): pl.pallas_call(lambda *refs: own_kernel(position(), *refs), out_shape=jax...  4.44 us
    pallas_call x3, Pallas kernels, whole_call(): pl.pallas_call(body, out_shape=[jax.ShapeDtypeStruct(o, F32) for o in out...  1.37 us
  transfers between devices with their start and end apart: 14, of which 7 were waited for; matrix products, arithmetic and copies ran while one was open for 0% of the time, Pallas kernels for 8%

profile of v5, /device:TPU:0, one launch (start us, length us, event | category | flops | bytes accessed | tf_op | source)
XLA Modules:
  0.0 53.2 jit_solution(8489274891887613583)
XLA Ops:
  0.7 11.0 %front.1 = (f32[300,2048]{1,0:T(8,128)}, f32[328,128]{1,0:T(8,128)}) custom-call(bf16[300,128]{1,0:T(8,128)(2,1)} %refs_0_.3, bf16[8,300]{1,0:T(8,128)(2,1)} %bitcast.3, bf16[1024,4096]{1,0:T(8,128)(2,1)} %bitcast.5, bf16[300,4096]{1,0:T(8,128)(2,1)} %refs_3_.3, bf16[128,2048]{1,0:T(8,128)(2,1)} %refs_4_.3), custom_call_target="tpu_custom_call" | custom-call | flops 4880793600 | bytes 10846208 | tf_op jit(solution)/shard_map/front/pallas_call | solution.py:167
  11.8 3.4 %collective-permute-start.1 = (f32[328,128]{1,0:T(8,128)}, f32[328,128]{1,0:T(8,128)S(1)}, u32[]{:S(2)}, u32[]{:S(2)}) collective-permute-start(f32[328,128]{1,0:T(8,128)} %get-tuple-element.22.refs_2_), channel_id=1, source_target_pairs={{0,4},{1,5},{2,6},{3,7},{4,0},{5,1},{6,2},{7,3},{8,12},{9,13},{10,... | collective-permute-start | bytes 503816 | tf_op jit(solution)/shard_map/ppermute | solution.py:347
  15.2 4.4 %own_half.1.refs_0_ = f32[300,2048]{1,0:T(8,128)S(1)} custom-call(bf16[300,128]{1,0:T(8,128)(2,1)S(1)} %copy-done.2, bf16[8,300]{1,0:T(8,128)(2,1)S(1)} %bitcast.4, bf16[1024,4096]{1,0:T(8,128)(2,1)} %bitcast.6, bf16[300,4096]{1,0:T(8,128)(2,1)} %refs_3_.3, bf16[128,2048]{1,0:T(8,128)(2,1)S(1)} %copy-done.1, f32[300,2048]{1,0:T(8,128)} %get-tuple-element.21.refs_5_), custom_call_target="tpu_custom_call" | custom-call | flops 19955712000 | bytes 78807040 | tf_op jit(solution)/shard_map/own_half/pallas_call | solution.py:228
  19.6 0.7 %collective-permute-done.1.refs_3_ = f32[328,128]{1,0:T(8,128)S(1)} collective-permute-done((f32[328,128]{1,0:T(8,128)}, f32[328,128]{1,0:T(8,128)S(1)}, u32[]{:S(2)}, u32[]{:S(2)}) %collective-permute-start.1) | collective-permute-done | bytes 167968 | tf_op jit(solution)/shard_map/ppermute | solution.py:347
  20.3 0.3 first_sum.1
  20.6 1.7 %collective-permute-start.5 = (f32[172,1024]{1,0:T(8,128)S(1)}, f32[172,1024]{1,0:T(8,128)S(1)}, u32[]{:S(2)}, u32[]{:S(2)}) collective-permute-start(f32[172,1024]{1,0:T(8,128)S(1)} %get-tuple-element.28), channel_id=1, source_target_pairs={{0,8},{8,0},{16,24},{24,16},{32,40},{40,32},{48,56},{56,48},{1,9},... | collective-permute-start | bytes 2113544 | tf_op jit(solution)/shard_map/ppermute | solution.py:347
  22.3 1.9 %collective-permute-start.6 = (f32[328,128]{1,0:T(8,128)S(1)}, f32[328,128]{1,0:T(8,128)S(1)}, u32[]{:S(2)}, u32[]{:S(2)}) collective-permute-start(f32[328,128]{1,0:T(8,128)S(1)} %get-tuple-element.29), channel_id=1, source_target_pairs={{0,1},{1,0},{2,3},{3,2},{4,5},{5,4},{6,7},{7,6},{8,9},{9,8},{10,11... | collective-permute-start | bytes 503816 | tf_op jit(solution)/shard_map/ppermute | solution.py:347
  24.2 1.5 %collective-permute-start.2 = (f32[128,512]{1,0:T(8,128)S(1)}, f32[128,512]{1,0:T(8,128)S(1)}, u32[]{:S(2)}, u32[]{:S(2)}) collective-permute-start(f32[128,512]{1,0:T(8,128)S(1)} %get-tuple-element.24), channel_id=1, source_target_pairs={{0,16},{8,24},{16,32},{24,40},{32,48},{40,56},{48,0},{56,8},{1,17}... | collective-permute-start | bytes 786440 | tf_op jit(solution)/shard_map/ppermute | solution.py:347
  25.7 2.7 %collective-permute-start.3 = (f32[128,512]{1,0:T(8,128)S(1)}, f32[128,512]{1,0:T(8,128)S(1)}, u32[]{:S(2)}, u32[]{:S(2)}) collective-permute-start(f32[128,512]{1,0:T(8,128)S(1)} %get-tuple-element.25), channel_id=1, source_target_pairs={{0,32},{8,40},{16,48},{24,56},{32,0},{40,8},{48,16},{56,24},{1,33}... | collective-permute-start | bytes 786440 | tf_op jit(solution)/shard_map/ppermute | solution.py:347
  28.4 1.4 %collective-permute-start.4 = (f32[128,512]{1,0:T(8,128)S(1)}, f32[128,512]{1,0:T(8,128)S(1)}, u32[]{:S(2)}, u32[]{:S(2)}) collective-permute-start(f32[128,512]{1,0:T(8,128)S(1)} %get-tuple-element.26), channel_id=1, source_target_pairs={{0,48},{8,56},{16,0},{24,8},{32,16},{40,24},{48,32},{56,40},{1,49}... | collective-permute-start | bytes 786440 | tf_op jit(solution)/shard_map/ppermute | solution.py:347
  29.9 3.7 %collective-permute-start.7 = (f32[328,128]{1,0:T(8,128)S(1)}, f32[328,128]{1,0:T(8,128)S(1)}, u32[]{:S(2)}, u32[]{:S(2)}) collective-permute-start(f32[328,128]{1,0:T(8,128)S(1)} %add.6), channel_id=1, source_target_pairs={{0,2},{1,3},{2,0},{3,1},{4,6},{5,7},{6,4},{7,5},{8,10},{9,11},{10,... | collective-permute-start | bytes 503816 | tf_op jit(solution)/shard_map/ppermute | solution.py:347
  33.6 3.3 %collective-permute-done.7 = f32[328,128]{1,0:T(8,128)S(1)} collective-permute-done((f32[328,128]{1,0:T(8,128)S(1)}, f32[328,128]{1,0:T(8,128)S(1)}, u32[]{:S(2)}, u32[]{:S(2)}) %collective-permute-start.7) | collective-permute-done | bytes 167968 | tf_op jit(solution)/shard_map/ppermute | solution.py:347
  36.9 0.5 %collective-permute-start.8 = (f32[24,128]{1,0:T(8,128)S(1)}, f32[24,128]{1,0:T(8,128)S(1)}, u32[]{:S(2)}, u32[]{:S(2)}) collective-permute-start(f32[24,128]{1,0:T(8,128)S(1)} %slice.4.refs_6_), channel_id=1, source_target_pairs={{0,8},{8,0},{16,24},{24,16},{32,40},{40,32},{48,56},{56,48},{1,9},... | collective-permute-start | bytes 36872 | tf_op jit(solution)/shard_map/ppermute | solution.py:347
  37.5 1.9 %collective-permute-done.3.refs_2_ = f32[128,512]{1,0:T(8,128)S(1)} collective-permute-done((f32[128,512]{1,0:T(8,128)S(1)}, f32[128,512]{1,0:T(8,128)S(1)}, u32[]{:S(2)}, u32[]{:S(2)}) %collective-permute-start.3) | collective-permute-done | bytes 262176 | tf_op jit(solution)/shard_map/ppermute | solution.py:347
  39.3 1.4 %collective-permute-done.8.refs_7_ = f32[24,128]{1,0:T(8,128)S(1)} collective-permute-done((f32[24,128]{1,0:T(8,128)S(1)}, f32[24,128]{1,0:T(8,128)S(1)}, u32[]{:S(2)}, u32[]{:S(2)}) %collective-permute-start.8) | collective-permute-done | bytes 12320 | tf_op jit(solution)/shard_map/ppermute | solution.py:347
  40.7 0.2 middle_sum.1
  40.9 0.7 %collective-permute-start.10 = (f32[200,256]{1,0:T(8,128)S(1)}, f32[200,256]{1,0:T(8,128)S(1)}, u32[]{:S(2)}, u32[]{:S(2)}) collective-permute-start(f32[200,256]{1,0:T(8,128)S(1)} %get-tuple-element.33), channel_id=1, source_target_pairs={{0,16},{8,24},{16,32},{24,40},{32,48},{40,56},{48,0},{56,8},{1,17}... | collective-permute-start | bytes 614408 | tf_op jit(solution)/shard_map/ppermute | solution.py:347
  41.6 1.9 %collective-permute-start.11 = (f32[200,256]{1,0:T(8,128)S(1)}, f32[200,256]{1,0:T(8,128)S(1)}, u32[]{:S(2)}, u32[]{:S(2)}) collective-permute-start(f32[200,256]{1,0:T(8,128)S(1)} %get-tuple-element.34), channel_id=1, source_target_pairs={{0,32},{8,40},{16,48},{24,56},{32,0},{40,8},{48,16},{56,24},{1,33}... | collective-permute-start | bytes 614408 | tf_op jit(solution)/shard_map/ppermute | solution.py:347
  43.5 1.4 %collective-permute-start.12 = (f32[200,256]{1,0:T(8,128)S(1)}, f32[200,256]{1,0:T(8,128)S(1)}, u32[]{:S(2)}, u32[]{:S(2)}) collective-permute-start(f32[200,256]{1,0:T(8,128)S(1)} %get-tuple-element.35), channel_id=1, source_target_pairs={{0,48},{8,56},{16,0},{24,8},{32,16},{40,24},{48,32},{56,40},{1,49}... | collective-permute-start | bytes 614408 | tf_op jit(solution)/shard_map/ppermute | solution.py:347
  44.9 1.2 %collective-permute-start.9 = (f32[128,256]{1,0:T(8,128)S(1)}, f32[128,256]{1,0:T(8,128)S(1)}, u32[]{:S(2)}, u32[]{:S(2)}) collective-permute-start(f32[128,256]{1,0:T(8,128)S(1)} %get-tuple-element.31), channel_id=1, source_target_pairs={{0,8},{8,0},{16,24},{24,16},{32,40},{40,32},{48,56},{56,48},{1,9},... | collective-permute-start | bytes 393224 | tf_op jit(solution)/shard_map/ppermute | solution.py:347
  46.2 0.1 collective-permute-done.13.refs_7_
  46.3 4.5 %collective-permute-done.9.refs_1_ = f32[128,256]{1,0:T(8,128)S(1)} collective-permute-done((f32[128,256]{1,0:T(8,128)S(1)}, f32[128,256]{1,0:T(8,128)S(1)}, u32[]{:S(2)}, u32[]{:S(2)}) %collective-permute-start.9) | collective-permute-done | bytes 131104 | tf_op jit(solution)/shard_map/ppermute | solution.py:347
  50.8 1.5 %collective-permute-done.11.refs_4_ = f32[200,256]{1,0:T(8,128)S(1)} collective-permute-done((f32[200,256]{1,0:T(8,128)S(1)}, f32[200,256]{1,0:T(8,128)S(1)}, u32[]{:S(2)}, u32[]{:S(2)}) %collective-permute-start.11) | collective-permute-done | bytes 204832 | tf_op jit(solution)/shard_map/ppermute | solution.py:347
  52.3 0.9 %last_sum.1 = (f32[300,256]{1,0:T(8,128)}, f32[300,128]{1,0:T(8,128)}, f32[8,300]{1,0:T(8,128)}) custom-call(f32[128,256]{1,0:T(8,128)S(1)} %get-tuple-element.30.refs_0_, f32[128,256]{1,0:T(8,128)S(1)} %collective-permute-done.9.refs_1_, f32[200,256]{1,0:T(8,128)S(1)} %get-tuple-element.32.refs_2_, f32[200,256]{1,0:T(8,128)S(1)} %collective-permute-done.10.refs_3_, ...), custom_call_target="tpu_custom_call" | custom-call | flops 1024 | bytes 1024 | tf_op jit(solution)/shard_map/last_sum/pallas_call | solution.py:253
  (20 shorter events, 0.2 us)
Async XLA Ops:
  0.6 14.5 %copy-start.1 = (bf16[128,2048]{1,0:T(8,128)(2,1)S(1)}, bf16[128,2048]{1,0:T(8,128)(2,1)}, u32[]{:S(2)}) copy-start(bf16[128,2048]{1,0:T(8,128)(2,1)} %refs_4_.3) | copy-start | bytes 1572868
  0.6 14.5 %copy-start.2 = (bf16[300,128]{1,0:T(8,128)(2,1)S(1)}, bf16[300,128]{1,0:T(8,128)(2,1)}, u32[]{:S(2)}) copy-start(bf16[300,128]{1,0:T(8,128)(2,1)} %refs_0_.3) | copy-start | bytes 230404
  0.7 14.5 %copy-start.3 = (bf16[300,8]{0,1:T(8,128)(2,1)S(1)}, bf16[300,8]{0,1:T(8,128)(2,1)}, u32[]{:S(2)}) copy-start(bf16[300,8]{0,1:T(8,128)(2,1)} %param.9) | copy-start | bytes 14404
  11.7 8.6 %collective-permute-start = (f32[300,2048]{1,0:T(8,128)}, f32[300,2048]{1,0:T(8,128)S(1)}, u32[]{:S(2)}, u32[]{:S(2)}) collective-permute-start(f32[300,2048]{1,0:T(8,128)} %get-tuple-element.21.refs_5_), channel_id=1, source_target_pairs={{0,64},{64,0},{1,65},{65,1},{2,66},{66,2},{3,67},{67,3},{4,68},{68... | collective-permute-start | bytes 7372808 | tf_op jit(solution)/shard_map/ppermute | solution.py:347
  11.8 8.5 %copy-start = (f32[328,128]{1,0:T(8,128)S(1)}, f32[328,128]{1,0:T(8,128)}, u32[]{:S(2)}) copy-start(f32[328,128]{1,0:T(8,128)} %get-tuple-element.22.refs_2_) | copy-start | bytes 503812
  11.8 8.5 %collective-permute-start.1 = (f32[328,128]{1,0:T(8,128)}, f32[328,128]{1,0:T(8,128)S(1)}, u32[]{:S(2)}, u32[]{:S(2)}) collective-permute-start(f32[328,128]{1,0:T(8,128)} %get-tuple-element.22.refs_2_), channel_id=1, source_target_pairs={{0,4},{1,5},{2,6},{3,7},{4,0},{5,1},{6,2},{7,3},{8,12},{9,13},{10,... | collective-permute-start | bytes 503816 | tf_op jit(solution)/shard_map/ppermute | solution.py:347
  20.6 20.1 %collective-permute-start.5 = (f32[172,1024]{1,0:T(8,128)S(1)}, f32[172,1024]{1,0:T(8,128)S(1)}, u32[]{:S(2)}, u32[]{:S(2)}) collective-permute-start(f32[172,1024]{1,0:T(8,128)S(1)} %get-tuple-element.28), channel_id=1, source_target_pairs={{0,8},{8,0},{16,24},{24,16},{32,40},{40,32},{48,56},{56,48},{1,9},... | collective-permute-start | bytes 2113544 | tf_op jit(solution)/shard_map/ppermute | solution.py:347
  22.3 7.6 %collective-permute-start.6 = (f32[328,128]{1,0:T(8,128)S(1)}, f32[328,128]{1,0:T(8,128)S(1)}, u32[]{:S(2)}, u32[]{:S(2)}) collective-permute-start(f32[328,128]{1,0:T(8,128)S(1)} %get-tuple-element.29), channel_id=1, source_target_pairs={{0,1},{1,0},{2,3},{3,2},{4,5},{5,4},{6,7},{7,6},{8,9},{9,8},{10,11... | collective-permute-start | bytes 503816 | tf_op jit(solution)/shard_map/ppermute | solution.py:347
  24.2 13.3 %collective-permute-start.2 = (f32[128,512]{1,0:T(8,128)S(1)}, f32[128,512]{1,0:T(8,128)S(1)}, u32[]{:S(2)}, u32[]{:S(2)}) collective-permute-start(f32[128,512]{1,0:T(8,128)S(1)} %get-tuple-element.24), channel_id=1, source_target_pairs={{0,16},{8,24},{16,32},{24,40},{32,48},{40,56},{48,0},{56,8},{1,17}... | collective-permute-start | bytes 786440 | tf_op jit(solution)/shard_map/ppermute | solution.py:347
  25.7 13.6 %collective-permute-start.3 = (f32[128,512]{1,0:T(8,128)S(1)}, f32[128,512]{1,0:T(8,128)S(1)}, u32[]{:S(2)}, u32[]{:S(2)}) collective-permute-start(f32[128,512]{1,0:T(8,128)S(1)} %get-tuple-element.25), channel_id=1, source_target_pairs={{0,32},{8,40},{16,48},{24,56},{32,0},{40,8},{48,16},{56,24},{1,33}... | collective-permute-start | bytes 786440 | tf_op jit(solution)/shard_map/ppermute | solution.py:347
  28.4 10.9 %collective-permute-start.4 = (f32[128,512]{1,0:T(8,128)S(1)}, f32[128,512]{1,0:T(8,128)S(1)}, u32[]{:S(2)}, u32[]{:S(2)}) collective-permute-start(f32[128,512]{1,0:T(8,128)S(1)} %get-tuple-element.26), channel_id=1, source_target_pairs={{0,48},{8,56},{16,0},{24,8},{32,16},{40,24},{48,32},{56,40},{1,49}... | collective-permute-start | bytes 786440 | tf_op jit(solution)/shard_map/ppermute | solution.py:347
  29.9 7.0 %collective-permute-start.7 = (f32[328,128]{1,0:T(8,128)S(1)}, f32[328,128]{1,0:T(8,128)S(1)}, u32[]{:S(2)}, u32[]{:S(2)}) collective-permute-start(f32[328,128]{1,0:T(8,128)S(1)} %add.6), channel_id=1, source_target_pairs={{0,2},{1,3},{2,0},{3,1},{4,6},{5,7},{6,4},{7,5},{8,10},{9,11},{10,... | collective-permute-start | bytes 503816 | tf_op jit(solution)/shard_map/ppermute | solution.py:347
  36.9 3.8 %collective-permute-start.8 = (f32[24,128]{1,0:T(8,128)S(1)}, f32[24,128]{1,0:T(8,128)S(1)}, u32[]{:S(2)}, u32[]{:S(2)}) collective-permute-start(f32[24,128]{1,0:T(8,128)S(1)} %slice.4.refs_6_), channel_id=1, source_target_pairs={{0,8},{8,0},{16,24},{24,16},{32,40},{40,32},{48,56},{56,48},{1,9},... | collective-permute-start | bytes 36872 | tf_op jit(solution)/shard_map/ppermute | solution.py:347
  40.9 9.9 %collective-permute-start.10 = (f32[200,256]{1,0:T(8,128)S(1)}, f32[200,256]{1,0:T(8,128)S(1)}, u32[]{:S(2)}, u32[]{:S(2)}) collective-permute-start(f32[200,256]{1,0:T(8,128)S(1)} %get-tuple-element.33), channel_id=1, source_target_pairs={{0,16},{8,24},{16,32},{24,40},{32,48},{40,56},{48,0},{56,8},{1,17}... | collective-permute-start | bytes 614408 | tf_op jit(solution)/shard_map/ppermute | solution.py:347
  41.6 10.8 %collective-permute-start.11 = (f32[200,256]{1,0:T(8,128)S(1)}, f32[200,256]{1,0:T(8,128)S(1)}, u32[]{:S(2)}, u32[]{:S(2)}) collective-permute-start(f32[200,256]{1,0:T(8,128)S(1)} %get-tuple-element.34), channel_id=1, source_target_pairs={{0,32},{8,40},{16,48},{24,56},{32,0},{40,8},{48,16},{56,24},{1,33}... | collective-permute-start | bytes 614408 | tf_op jit(solution)/shard_map/ppermute | solution.py:347
  43.5 8.9 %collective-permute-start.12 = (f32[200,256]{1,0:T(8,128)S(1)}, f32[200,256]{1,0:T(8,128)S(1)}, u32[]{:S(2)}, u32[]{:S(2)}) collective-permute-start(f32[200,256]{1,0:T(8,128)S(1)} %get-tuple-element.35), channel_id=1, source_target_pairs={{0,48},{8,56},{16,0},{24,8},{32,16},{40,24},{48,32},{56,40},{1,49}... | collective-permute-start | bytes 614408 | tf_op jit(solution)/shard_map/ppermute | solution.py:347
  44.9 1.4 %collective-permute-start.13 = (f32[328,128]{1,0:T(8,128)S(1)}, f32[328,128]{1,0:T(8,128)S(1)}, u32[]{:S(2)}, u32[]{:S(2)}) collective-permute-start(f32[328,128]{1,0:T(8,128)S(1)} %add.7.refs_6_), channel_id=1, source_target_pairs={{0,64},{64,0},{1,65},{65,1},{2,66},{66,2},{3,67},{67,3},{4,68},{68... | collective-permute-start | bytes 503816 | tf_op jit(solution)/shard_map/ppermute | solution.py:347
  44.9 5.9 %collective-permute-start.9 = (f32[128,256]{1,0:T(8,128)S(1)}, f32[128,256]{1,0:T(8,128)S(1)}, u32[]{:S(2)}, u32[]{:S(2)}) collective-permute-start(f32[128,256]{1,0:T(8,128)S(1)} %get-tuple-element.31), channel_id=1, source_target_pairs={{0,8},{8,0},{16,24},{24,16},{32,40},{40,32},{48,56},{56,48},{1,9},... | collective-permute-start | bytes 393224 | tf_op jit(solution)/shard_map/ppermute | solution.py:347
